TPU v7x, 512 devices: a whole 4x4x16 slice. The times are simulated.
512 devices in a mesh: var: 16 (over z_lo, y), seq: 32 (over z_hi, x, core).
Axes of the slice: x: 4, y: 4, z: 16 (z_hi: 4, z_lo: 4; z = z_hi * 4 + z_lo), core: 2. Of those that a mesh axis runs over, the one named last changes fastest.
Arguments:
- pixels: bfloat16 [96, 4, 4096], P('var', None, 'seq'), may hold values from -6 to 6
- w_embed: bfloat16 [96, 4, 4096], P('var'), may hold values from -3 to 3
- var_embed: bfloat16 [96, 4096], P('var'), may hold values from -6 to 6
- var_mask: int32 [96], replicated, may hold values from 0 to 1, as said below
- agg_query: bfloat16 [4096], P('var')
- ln_gain: bfloat16 [4096], replicated, may hold values from 0.099609375 to 1.8984375
- w_up: bfloat16 [4096, 8192], P('seq', 'var'), may hold values from -0.09375 to 0.09375
- w_down: bfloat16 [8192, 4096], P('var', 'seq'), may hold values from -0.0625 to 0.0625
Outputs:
- mixed: bfloat16 [4096, 4096], P('seq', 'var')
Inputs may be any that keep to these rules, and one draw needn't show every extreme that they name: `var_mask`: exactly 91 entries are 1, the others 0.
All inputs are finite; a program needn't handle non-finite values.
Results may differ from a plain program's by a relative error of at most 0.025.
Values may be sent and summed in bfloat16 or wider, within the bound.
A program may use at most 64 MiB of HBM per device.

v0:
```python
import math

import jax
import jax.numpy as jnp
from jax import lax
from jax.sharding import PartitionSpec as P

PIX = 4
HS = 128


def aggregate_local(embedded, query_local, var_mask):
    count = embedded.shape[1]
    local_heads = query_local.shape[0] // HS
    parts = embedded.reshape(embedded.shape[0], count, local_heads, HS)
    query = query_local.reshape(local_heads, HS)
    scores = jnp.einsum(
        "vthd,hd->vht", parts, query, preferred_element_type=jnp.float32
    ) / math.sqrt(HS)
    scores = jnp.where(var_mask[:, None, None] > 0, scores, -1e30)
    top = jnp.max(scores, axis=0, keepdims=True)
    expo = jnp.exp(scores - top)
    weights = (expo / jnp.sum(expo, axis=0, keepdims=True)).astype(jnp.bfloat16)
    merged = jnp.einsum("vht,vthd->thd", weights, parts, preferred_element_type=jnp.float32)
    return merged.reshape(count, local_heads * HS).astype(jnp.bfloat16)


def shards(pixels, w_embed, var_embed, var_mask, agg_query, ln_gain, w_up, w_down):
    all_pixels = lax.all_gather(pixels, "var", axis=0, tiled=True)
    table = jnp.concatenate([w_embed, var_embed[:, None, :]], axis=1)
    columns = lax.all_to_all(table, "var", split_axis=2, concat_axis=0, tiled=True)
    embedded = (
        jnp.einsum(
            "vpt,vpc->vtc", all_pixels, columns[:, :PIX, :], preferred_element_type=jnp.float32
        )
        + columns[:, PIX, :][:, None, :]
    ).astype(jnp.bfloat16)
    aggregated = aggregate_local(embedded, agg_query, var_mask)
    whole = lax.all_gather(aggregated, "var", axis=1, tiled=True)
    values = whole.astype(jnp.float32)
    mean = jnp.mean(values, axis=1, keepdims=True)
    centered = values - mean
    variance = jnp.mean(centered * centered, axis=1, keepdims=True)
    normed = (centered * lax.rsqrt(variance + 1e-05) * ln_gain.astype(jnp.float32)).astype(
        jnp.bfloat16
    )
    pre_act = jnp.dot(
        normed, lax.all_gather(w_up, "seq", axis=0, tiled=True), preferred_element_type=jnp.float32
    )
    hidden = jax.nn.gelu(pre_act, approximate=True).astype(jnp.bfloat16)
    terms = jnp.dot(
        hidden,
        lax.all_gather(w_down, "seq", axis=1, tiled=True),
        preferred_element_type=jnp.float32,
    )
    update = lax.psum_scatter(
        terms.astype(jnp.bfloat16), "var", scatter_dimension=1, tiled=True
    ).astype(jnp.float32)
    return (aggregated.astype(jnp.float32) + update).astype(jnp.bfloat16)


def solution(mesh):
    return jax.shard_map(
        shards,
        mesh=mesh,
        in_specs=(
            P("var", None, "seq"),
            P("var", None, None),
            P("var", None),
            P(),
            P("var"),
            P(),
            P("seq", "var"),
            P("var", "seq"),
        ),
        out_specs=P("seq", "var"),
        check_vma=False,
    )
```

profile of v0, /device:TPU:6, one launch (start us, length us, event | category | flops | bytes accessed | tf_op | source)
XLA Modules:
  0.0 498.9 jit_solution(17170666941013661559)
XLA Ops:
  6.5 0.0 copy-start
  6.5 0.0 copy-start.2
  6.5 8.1 %copy.26 = bf16[6,4,4096]{1,0,2:T(8,128)(2,1)} copy(bf16[6,4,4096]{2,1,0:T(4,128)(2,1)} %param.9) | data formatting | bytes 393216 | tf_op args[1]
  14.7 0.0 copy-done.2
  14.7 7.3 %copy.27 = bf16[6,1,4096]{1,0,2:T(8,128)(2,1)} copy(bf16[6,1,4096]{2,0,1:T(8,128)(2,1)S(1)} %bitcast.51) | data formatting | bytes 98304 | tf_op jit(solution)/shard_map/broadcast_in_dim | solution.py:30
  22.0 11.6 %fusion.57 = bf16[4096,6,5]{2,1,0:T(8,128)(2,1)} fusion(bf16[6,1,4096]{1,0,2:T(8,128)(2,1)} %copy.27, bf16[6,4,4096]{1,0,2:T(8,128)(2,1)} %copy.26), kind=kLoop, calls=%fused_computation.62 | loop fusion | flops 491520 | bytes 491520
  33.6 0.0 copy-start.4
  33.6 0.0 copy-start.5
  33.6 10.9 %reshape.32 = bf16[16,2,3840]{2,1,0:T(2,128)(2,1)} reshape(bf16[4096,6,5]{2,1,0:T(8,128)(2,1)} %fusion.57) | data formatting | bytes 491520
  44.5 8.6 %all-to-all-start = ((bf16[16,2,3840]{2,1,0:T(2,128)(2,1)}), bf16[16,2,3840]{2,1,0:T(2,128)(2,1)S(1)}, u32[]{:S(2)}, u32[]{:S(2)}) async-start(bf16[16,2,3840]{2,1,0:T(2,128)(2,1)} %reshape.32), calls=%async_computation | async-start | bytes 491520 | tf_op jit(solution)/shard_map/all_to_all | solution.py:31
  53.2 0.0 all-gather.4.cloned.1.call-start
  53.2 0.0 copy-done.4
  53.3 43.1 %all_gather.12 = bf16[96,4,128]{2,1,0:T(4,128)(2,1)S(1)} all-gather(bf16[6,4,128]{2,1,0:T(4,128)(2,1)S(1)} %copy-done.4), channel_id=1, replica_groups=mesh['var'=16,'seq'=32] {'var'}, dimensions={0}, use_global_device_ids=true | all-gather | bytes 104448 | tf_op jit(solution)/shard_map/all_gather | solution.py:29
  96.3 0.0 copy-done.5
  96.3 0.0 all-to-all-done
  96.3 8.1 %reshape.33 = bf16[4096,6,5]{2,1,0:T(8,128)(2,1)} reshape(bf16[16,2,3840]{2,1,0:T(2,128)(2,1)S(1)} %all-to-all-done) | data formatting | bytes 491520
  104.5 7.9 %copy.29 = bf16[16,6,5,256]{3,2,1,0:T(8,128)(2,1)S(1)} copy(bf16[16,6,5,256]{2,1,3,0:T(8,128)(2,1)} %bitcast.42) | data formatting | bytes 491520 | tf_op jit(solution)/shard_map/all_to_all | solution.py:31
  112.4 0.1 slice_convert_fusion
  112.5 5.8 %add_convert_fusion = bf16[96,256,128]{2,1,0:T(8,128)(2,1)S(1)} fusion(f32[96,256]{1,0:T(8,128)S(1)} %bitcast.49, bf16[96,4,128]{2,1,0:T(4,128)(2,1)S(1)} %all_gather.12, bf16[96,5,256]{2,1,0:T(8,128)(2,1)S(1)} %bitcast.46), kind=kOutput, calls=%fused_computation.3 | convolution fusion | flops 31457280 | bytes 6684672 | tf_op jit(solution)/shard_map/vpt,vpc->vtc/dot_general | solution.py:33
  118.3 0.0 copy-start.1
  118.3 0.0 copy-done
  118.3 2.6 copy-done.1
  121.0 0.0 copy-start.3
  121.0 0.9 fusion.2
  121.9 0.1 fusion.14
  122.0 0.1 copy.44
  122.1 4.4 multiply_reduce_fusion
  126.5 0.1 copy.47
  126.6 0.6 copy.57
  127.2 0.0 all-gather.4.cloned.1.call-update
  127.3 0.0 all-gather.6.cloned.1.call-start
  127.3 0.7 all-gather.6.cloned.1.call-update
  128.0 0.0 all-gather.8.cloned.1.call-start
  128.1 0.7 all-gather.8.cloned.1.call-update
  128.7 0.0 reduce-scatter.2.cloned.1.call-start
  128.8 0.0 copy-done.3
  128.8 70.7 %all-gather.4.cloned.1.call-done = bf16[128,4096]{1,0:T(8,128)(2,1)} async-done(((bf16[128,256]{1,0:T(8,128)(2,1)}), bf16[128,4096]{1,0:T(8,128)(2,1)}) %all-gather.4.cloned.1.call-update) | async-done | bytes 1048592 | tf_op jit(solution)/shard_map/all_gather | solution.py:39
  199.5 1.5 convert_reduce_fusion
  201.0 1.7 fusion.6
  202.6 94.5 %all-gather.6.cloned.1.call-done = bf16[4096,512]{1,0:T(8,128)(2,1)} async-done(((bf16[128,512]{1,0:T(8,128)(2,1)}), bf16[4096,512]{1,0:T(8,128)(2,1)}) %all-gather.6.cloned.1.call-update) | async-done | bytes 4194320 | tf_op jit(solution)/shard_map/all_gather | solution.py:48
  297.2 102.8 %all-gather.8.cloned.1.call-done = bf16[512,4096]{1,0:T(8,128)(2,1)} async-done(((bf16[512,128]{1,0:T(8,128)(2,1)}), bf16[512,4096]{1,0:T(8,128)(2,1)}) %all-gather.8.cloned.1.call-update) | async-done | bytes 4194320 | tf_op jit(solution)/shard_map/all_gather | solution.py:53
  400.0 6.3 %convolution_convert_fusion = bf16[128,4096]{1,0:T(8,128)(2,1)} fusion(bf16[512,4096]{1,0:T(8,128)(2,1)} %all-gather.8.cloned.1.call-done, bf16[4096,512]{1,0:T(8,128)(2,1)} %all-gather.6.cloned.1.call-done, bf16[128,4096]{1,0:T(8,128)(2,1)} %all-gather.4.cloned.1.call-done, f32[4096]{0:T(1024)S(1)} %convert_element_type.47, f32[128]{0:T(128)S(1)} %add_rsqrt_fusion, ...), kind=kOutput, calls=%fused_computation.7 | convolution fusion | flops 1077477376 | bytes 10503168 | tf_op jit(solution)/shard_map/dot_general | solution.py:51
  406.3 0.0 reduce-scatter.2.cloned.1.call-update
  406.3 84.6 %reduce-scatter.2.cloned.1.call-done = bf16[128,256]{1,0:T(8,128)(2,1)} async-done(((bf16[128,4096]{1,0:T(8,128)(2,1)}), bf16[128,256]{1,0:T(8,128)(2,1)}) %reduce-scatter.2.cloned.1.call-update) | async-done | bytes 65552 | tf_op jit(solution)/shard_map/reduce_scatter | solution.py:56
  490.9 1.5 add_convert_fusion.1
  (5 shorter events, 0.0 us)
Async XLA Ops:
  6.5 111.8 %copy-start = (bf16[256]{0:T(256)(128)(2,1)S(1)}, bf16[256]{0:T(256)(128)(2,1)}, u32[]{:S(2)}) copy-start(bf16[256]{0:T(256)(128)(2,1)} %param.12) | copy-start | bytes 1540
  6.5 8.1 %copy-start.2 = (bf16[6,4096]{1,0:T(8,128)(2,1)S(1)}, bf16[6,4096]{1,0:T(8,128)(2,1)}, u32[]{:S(2)}) copy-start(bf16[6,4096]{1,0:T(8,128)(2,1)} %param.10) | copy-start | bytes 147460
  33.6 19.6 %copy-start.4 = (bf16[6,4,128]{2,1,0:T(4,128)(2,1)S(1)}, bf16[6,4,128]{2,1,0:T(4,128)(2,1)}, u32[]{:S(2)}) copy-start(bf16[6,4,128]{2,1,0:T(4,128)(2,1)} %param.8) | copy-start | bytes 18436
  33.6 62.7 %copy-start.5 = (s32[96]{0:T(128)S(1)}, s32[96]{0:T(128)}, u32[]{:S(2)}) copy-start(s32[96]{0:T(128)} %param.11) | copy-start | bytes 1156
  44.5 51.8 %all-to-all-start = ((bf16[16,2,3840]{2,1,0:T(2,128)(2,1)}), bf16[16,2,3840]{2,1,0:T(2,128)(2,1)S(1)}, u32[]{:S(2)}, u32[]{:S(2)}) async-start(bf16[16,2,3840]{2,1,0:T(2,128)(2,1)} %reshape.32), calls=%async_computation | async-start | bytes 491520 | tf_op jit(solution)/shard_map/all_to_all | solution.py:31
  53.2 146.3 %all-gather.4.cloned.1.call-start = ((), (), s32[]{:S(2)}) async-start(), calls=%async_computation.2 | async-start | bytes 1114112 | tf_op jit(solution)/shard_map/all_gather | solution.py:39
  118.3 2.6 copy-start.1
  121.0 7.8 %copy-start.3 = (bf16[4096]{0:T(1024)(128)(2,1)S(1)}, bf16[4096]{0:T(1024)(128)(2,1)}, u32[]{:S(2)}) copy-start(bf16[4096]{0:T(1024)(128)(2,1)} %param.13) | copy-start | bytes 24580
  127.3 169.9 %all-gather.6.cloned.1.call-start = ((), (), s32[]{:S(2)}) async-start(), calls=%async_computation.3 | async-start | bytes 4325376 | tf_op jit(solution)/shard_map/all_gather | solution.py:48
  128.0 272.0 %all-gather.8.cloned.1.call-start = ((), (), s32[]{:S(2)}) async-start(), calls=%async_computation.4 | async-start | bytes 4325376 | tf_op jit(solution)/shard_map/all_gather | solution.py:53
  128.7 362.1 %reduce-scatter.2.cloned.1.call-start = ((), (), s32[]{:S(2)}) async-start(), calls=%async_computation.5 | async-start | bytes 1114112 | tf_op jit(solution)/shard_map/reduce_scatter | solution.py:56
Sparse Core Ops, SparseCore 0:
  127.4 72.0 all-gather.3
  202.6 94.4 all-gather.5
  300.2 99.7 all-gather.7
  406.4 84.4 reduce-scatter.1
where the time goes:
time: 500 us; the launch traced here: 499 us
  waiting for transfers between devices  354 us (71%)
  local copies, waits for them, and re-layouts  46 us (9%)
  blocking collectives  43.1 us (9%)
  other arithmetic  20.8 us (4%)
  between operations  13.2 us (3%)
  matrix products  13 us (3%)
  starting transfers between devices  8.8 us (2%)
    all_gather x1, waiting for transfers between devices, shards(): lax.all_gather(w_down, 'seq', axis=1, tiled=True)  103 us
    all_gather x1, waiting for transfers between devices, shards(): lax.all_gather(w_up, 'seq', axis=0, tiled=True)  94.5 us
    reduce_scatter x1, waiting for transfers between devices, shards(): lax.psum_scatter(terms.astype(jnp.bfloat16), 'var', scatter_dimension=1,...  84.6 us
    all_gather x1, waiting for transfers between devices, shards(): whole = lax.all_gather(aggregated, 'var', axis=1, tiled=True)  70.7 us
    all_gather x1, blocking collectives, shards(): all_pixels = lax.all_gather(pixels, 'var', axis=0, tiled=True)  43.1 us
    unnamed x19, local copies, waits for them, and re-layouts  30.7 us
    unnamed x2, other arithmetic  15.9 us
  transfers between devices with their start and end apart: 5, of which 4 were waited for; matrix products, arithmetic and copies ran while one was open for 1% of the time, Pallas kernels for 0%

commit v1 on v0

v1 whole, which is shorter than its diff:
```python
import math

import jax
import jax.numpy as jnp
from jax import lax
from jax.experimental import pallas as pl
from jax.experimental.pallas import tpu as pltpu
from jax.sharding import PartitionSpec as P

MESH = pl.DeviceIdType.MESH
F32, BF16 = jnp.float32, jnp.bfloat16
PIX, HS = 4, 128
N_VARS = 96
OWN_VARS = 6
ROWS = 32
DEPTH = 16 * ROWS
TOK, COLS, D, FF = 128, 256, 4096, 512
N_SEMS = 224


def block_of(iota):
    block, row = iota // ROWS, iota % ROWS
    owner = (block % 4) * 4 + block // 4
    local = jnp.where(row < OWN_VARS * PIX, row // PIX, row - OWN_VARS * PIX)
    return owner * OWN_VARS + local, row < OWN_VARS * (PIX + 1)


def kernel(
    pix_in, emb_in, bias_in, mask_in, query_in, gain_in, up_in, down_in, out,
    pix, emb, bias, mask, query, gain, rows_f, pix_f,
    tab_out, tab_mid, tab, pat, agg, norm, up, down, own_sum, term, got_y, got_z, part, total,
    local_sem, send_sem, recv_sem,
):
    var, seq = lax.axis_index("var"), lax.axis_index("seq")
    zl, y = var // 4, lax.rem(var, 4)
    zh, x, core = seq // 8, lax.rem(seq // 2, 4), lax.rem(seq, 2)
    z = zh * 4 + zl
    other = 1 - core

    def mod4(v):
        return lax.rem(v + 4, 4)

    def at_var(zl_, y_):
        return (zl_ * 4 + y_, seq)

    def at_seq(a, b, core_):
        return (var, mod4(zh + a) * 8 + mod4(x + b) * 2 + core_)

    def at_z(d):
        z_ = lax.rem(z + d + 16, 16)
        return (lax.rem(z_, 4) * 4 + y, (z_ // 4) * 8 + x * 2 + core)

    sibling = at_seq(0, 0, other)

    locals_ = []
    for i, (src, dst) in enumerate(
        (
            (pix_in, pix),
            (emb_in, emb),
            (bias_in, bias),
            (mask_in, mask),
            (query_in, query),
            (gain_in, gain),
            (up_in, up.at[zh, x * 2 + core]),
            (down_in, down.at[zh, x, :, pl.ds(pl.multiple_of(core * HS, HS), HS)]),
        )
    ):
        locals_.append(pltpu.make_async_copy(src, dst, local_sem.at[i]))
        locals_[-1].start()

    barrier = pltpu.get_barrier_semaphore()
    peers = [at_z(1), at_z(-1), at_z(2), at_z(-2), sibling]
    peers += [at_var(mod4(zl + i), y) for i in (1, 2, 3)]
    peers += [at_var(zl, mod4(y + i)) for i in (1, 2, 3)]
    peers += [at_seq(1, 0, core), at_seq(-1, 0, core), at_seq(0, 1, core), at_seq(0, -1, core)]
    for peer in peers:
        pl.semaphore_signal(barrier, inc=1, device_id=peer, device_id_type=MESH)

    sends, keys = [], {}

    def sem_of(key):
        return keys.setdefault(key, len(keys))

    def copy_of(src, dst, index, device):
        copy = pltpu.make_async_remote_copy(
            src_ref=src,
            dst_ref=dst,
            send_sem=send_sem.at[len(sends)],
            recv_sem=recv_sem.at[index],
            device_id=device,
            device_id_type=MESH,
        )
        return copy

    def send(src, dst, key, device):
        copy = copy_of(src, dst, sem_of(key), device)
        copy.start()
        sends.append(copy)

    def recv(dst, key):
        pltpu.make_async_remote_copy(
            src_ref=dst,
            dst_ref=dst,
            send_sem=send_sem.at[0],
            recv_sem=recv_sem.at[sem_of(key)],
            device_id=sibling,
            device_id_type=MESH,
        ).wait_recv()

    for i in range(3):
        locals_[i].wait()
    rows_f[:, OWN_VARS * (PIX + 1) :, :] = jnp.zeros((16, ROWS - OWN_VARS * (PIX + 1), HS), F32)
    for j in range(16):
        col = pl.ds(pl.multiple_of(j * COLS + core * HS, HS), HS)
        for v in range(OWN_VARS):
            rows_f[j, v * PIX : (v + 1) * PIX, :] = emb[v, :, col].astype(F32)
        rows_f[j, OWN_VARS * PIX : OWN_VARS * (PIX + 1), :] = bias[:, col].astype(F32)
    for j in range(16):
        tab_out[j // 4, j % 4] = rows_f[j].astype(BF16)
    row = lax.broadcasted_iota(jnp.int32, (ROWS, TOK), 0)
    pix_f[...] = jnp.where(row < OWN_VARS * (PIX + 1), 1.0, 0.0)
    for v in range(OWN_VARS):
        pix_f[v * PIX : (v + 1) * PIX, :] = pix[v].astype(F32)
    pat[y, zl] = pix_f[...].astype(BF16)

    pl.semaphore_wait(barrier, len(peers))

    for i in (1, 2, 3):
        send(pat.at[y, zl], pat.at[y, zl], ("pz", i), at_var(mod4(zl + i), y))
    for i, step in ((1, 1), (3, -1), (2, 2 - 4 * core)):
        send(tab_out.at[mod4(zl + i)], tab_mid.at[zl], ("tz", i), at_z(step))

    def part_of(m, a, b, core_, half):
        if m == 0:
            ref = up.at[mod4(zh + a), mod4(x + b) * 2 + core_]
            return ref if half is None else ref.at[pl.ds(half * 64, 64)]
        rows = pl.ds(0, FF) if half is None else pl.ds(half * 256, 256)
        cols = pl.ds(pl.multiple_of(core_ * HS, HS), HS)
        return down.at[mod4(zh + a), mod4(x + b), rows, cols]

    def weight(m, a, b, half, way):
        da, db = {"z+": (1, 0), "z-": (-1, 0), "x+": (0, 1), "x-": (0, -1), "s": (0, 0)}[way]
        place = part_of(m, a, b, core, half)
        src = place
        if a == 0 and b == 0:
            src = (up_in, down_in)[m]
            if half is not None:
                src = src.at[pl.ds(half * (64, 256)[m], (64, 256)[m])]
        key = ("w", m, (a - da) % 4, (b - db) % 4, way == "s", half)
        send(src, place, key, at_seq(da, db, other if way == "s" else core))

    def weight_here(m, a, b, half=None, swapped=False):
        recv(part_of(m, a, b, other if swapped else core, half), ("w", m, a % 4, b % 4, swapped, half))

    def first(m):
        weight(m, 0, 0, 0, "z+")
        weight(m, 0, 0, 1, "z-")
        weight(m, 0, 0, 1, "z+")
        weight(m, 0, 0, 0, "z-")
        spread(m, 0)

    def spread(m, a):
        weight(m, a, 0, None, "x+")
        weight(m, a, 0, None, "x-")
        weight(m, a, 0, None, "s")

    def x_near(m, a):
        weight_here(m, a, -1)
        weight(m, a, -1, 0, "x+")
        weight(m, a, -1, None, "s")
        weight_here(m, a, 1)
        weight(m, a, 1, 1, "x-")
        weight(m, a, 1, None, "s")

    def x_far(m, a):
        weight_here(m, a, 2, 0)
        weight_here(m, a, 2, 1)
        weight(m, a, 2, None, "s")

    def z_near(m):
        weight_here(m, -1, 0, 0)
        weight(m, -1, 0, 0, "z+")
        weight_here(m, 1, 0, 1)
        weight(m, 1, 0, 1, "z-")

    def z_near_rest(m):
        weight_here(m, -1, 0, 1)
        spread(m, -1)
        weight_here(m, 1, 0, 0)
        spread(m, 1)

    def z_far(m):
        weight_here(m, 2, 0, 0)
        weight_here(m, 2, 0, 1)
        spread(m, 2)

    def swapped(m, a):
        for b in range(4):
            weight_here(m, a, b, None, True)

    first(0)
    tab_mid[zl] = tab_out[zl]

    for i in (1, 2, 3):
        recv(pat.at[y, mod4(zl - i)], ("pz", i))
    for i in (1, 2, 3):
        send(pat.at[y], pat.at[y], ("py", i), at_var(zl, mod4(y + i)))
    for i in (1, 2, 3):
        recv(tab_mid.at[mod4(zl - i)], ("tz", i))
    for i in (1, 2, 3):
        y_ = mod4(y + i)
        send(tab_mid.at[:, y_], tab.at[core, y], ("ty", i), at_var(zl, y_))
    tab[core, y] = tab_mid[:, y]
    for i in (1, 2, 3):
        recv(tab.at[core, mod4(y - i)], ("ty", i))
    send(tab.at[core], tab.at[core], "ts", sibling)
    for i in (1, 2, 3):
        recv(pat.at[mod4(y - i)], ("py", i))
    recv(tab.at[other], "ts")

    locals_[3].wait()
    locals_[4].wait()
    points = pat[...].reshape(DEPTH, TOK)
    points_f = points.astype(F32)
    twice = jnp.concatenate([points_f, points_f], axis=1)
    query_f = query[...].astype(F32).reshape(1, COLS)
    tables = [tab[h].reshape(DEPTH, HS) for h in range(2)]
    shares = []
    for h in range(2):
        dots = jnp.sum(tables[h].astype(F32) * query_f[:, h * HS : (h + 1) * HS], axis=1, keepdims=True)
        shares.append((dots * (1.0 / math.sqrt(HS))) * points_f)
    share = jnp.concatenate(shares, axis=1)
    which, real = block_of(lax.broadcasted_iota(jnp.int32, (N_VARS, DEPTH), 1))
    collect = jnp.where(
        (which == lax.broadcasted_iota(jnp.int32, (N_VARS, DEPTH), 0)) & real, 1.0, 0.0
    ).astype(BF16)
    scores = jnp.zeros((N_VARS, COLS), F32)
    for _ in range(3):
        piece = share.astype(BF16)
        share = share - piece.astype(F32)
        scores = scores + jnp.dot(collect, piece, preferred_element_type=F32)
    diagonal = lax.broadcasted_iota(jnp.int32, (N_VARS, N_VARS), 0) == lax.broadcasted_iota(
        jnp.int32, (N_VARS, N_VARS), 1
    )
    keep = jnp.sum(
        jnp.where(diagonal, mask[...].astype(F32).reshape(1, N_VARS), 0.0), axis=1, keepdims=True
    )
    scores = jnp.where(keep > 0.0, scores, -1e30)
    expo = jnp.exp(scores - jnp.max(scores, axis=0, keepdims=True))
    weights = (expo / jnp.sum(expo, axis=0, keepdims=True)).astype(BF16)
    which, real = block_of(lax.broadcasted_iota(jnp.int32, (DEPTH, N_VARS), 0))
    expand = jnp.where(
        (which == lax.broadcasted_iota(jnp.int32, (DEPTH, N_VARS), 1)) & real, 1.0, 0.0
    ).astype(BF16)
    mixed = jnp.dot(expand, weights, preferred_element_type=F32) * twice
    high = mixed.astype(BF16)
    low = (mixed - high.astype(F32)).astype(BF16)
    over_rows = (((0,), (0,)), ((), ()))
    merged = []
    for h in range(2):
        cols = slice(h * HS, (h + 1) * HS)
        merged.append(
            lax.dot_general(high[:, cols], tables[h], over_rows, preferred_element_type=F32)
            + lax.dot_general(low[:, cols], tables[h], over_rows, preferred_element_type=F32)
        )
    agg[var] = jnp.concatenate(merged, axis=1).astype(BF16)

    for i in (1, 2, 3):
        send(agg.at[var], agg.at[var], ("az", i), at_var(mod4(zl + i), y))
    for i in (1, 3, 2):
        send(agg.at[var], agg.at[var], ("ay", 0, i), at_var(zl, mod4(y + i)))
    x_near(0, 0)
    z_near(0)
    first(1)
    for j in (1, 2, 3):
        place = agg.at[mod4(zl - j) * 4 + y]
        recv(place, ("az", j))
        for i in (1, 3, 2):
            send(place, place, ("ay", j, i), at_var(zl, mod4(y + i)))
    z_near_rest(0)
    x_far(0, 0)
    x_near(1, 0)
    for j in range(4):
        for i in (1, 3, 2):
            recv(agg.at[mod4(zl - j) * 4 + mod4(y - i)], ("ay", j, i))

    def row_sum(v, acc):
        return acc + jnp.sum(agg[v].astype(F32), axis=1, keepdims=True)

    mean = lax.fori_loop(0, 16, row_sum, jnp.zeros((TOK, 1), F32)) * (1.0 / D)

    def square_sum(v, acc):
        centered = agg[v].astype(F32) - mean
        return acc + jnp.sum(centered * centered, axis=1, keepdims=True)

    variance = lax.fori_loop(0, 16, square_sum, jnp.zeros((TOK, 1), F32)) * (1.0 / D)
    scale = lax.rsqrt(variance + 1e-05)
    locals_[5].wait()
    for v in range(16):
        cols = slice(v * COLS, (v + 1) * COLS)
        gains = gain[cols].astype(F32).reshape(1, COLS)
        norm[v // 4, :, (v % 4) * COLS : (v % 4 + 1) * COLS] = (
            (agg[v].astype(F32) - mean) * scale * gains
        ).astype(BF16)

    x_near(0, -1)
    x_near(0, 1)
    z_far(0)
    x_far(0, -1)
    x_far(0, 1)
    z_near(1)
    x_near(0, 2)
    x_far(1, 0)

    locals_[6].wait()

    def up_part(a):
        swapped(0, a)
        q = mod4(zh + a)
        return jnp.dot(norm[q], up[q].reshape(1024, FF), preferred_element_type=F32)

    part[...] = up_part(0)
    part[...] += up_part(-1)
    part[...] += up_part(1)
    x_far(0, 2)
    z_near_rest(1)
    hidden = jax.nn.gelu(part[...] + up_part(2), approximate=True).astype(BF16)

    def down_part(a):
        q = mod4(zh + a)
        swapped(1, a)
        for i in (2, 1, 3, 0):
            y_ = mod4(y + i)
            value = jnp.dot(hidden, down[q, y_], preferred_element_type=F32)
            if i == 0:
                own_sum[a % 4] = value
            else:
                term[a % 4, i] = value.astype(BF16)
                send(term.at[a % 4, i], got_y.at[a % 4, i], ("ry", a % 4, i), at_var(zl, y_))

    optional = []

    def down_sum(a):
        a = a % 4
        q = mod4(zh + a)
        value = own_sum[a]
        for i in (1, 2, 3):
            recv(got_y.at[a, i], ("ry", a, i))
            value = value + got_y[a, i].astype(F32)
        mine = zl == q
        away = mod4(zl - q)
        base = sem_of(("rz", 1))
        assert [sem_of(("rz", i)) for i in (1, 2, 3)] == [base, base + 1, base + 2]

        @pl.when(mine)
        def _():
            total[...] = value

        copy = copy_of(
            own_bf.at[a], got_z.at[away], base + lax.rem(away + 2, 3), at_var(q, y)
        )
        sends.append(None)

        @pl.when(jnp.logical_not(mine))
        def _():
            own_bf[a] = value.astype(BF16)
            copy.start()

        optional.append((mine, copy))

    own_bf = term.at[:, 0]
    locals_[7].wait()
    down_part(0)
    x_near(1, -1)
    x_near(1, 1)
    down_sum(0)
    z_far(1)
    x_far(1, -1)
    x_far(1, 1)
    down_part(-1)
    down_part(1)
    x_near(1, 2)
    down_sum(-1)
    down_sum(1)
    x_far(1, 2)
    down_part(2)
    for copy in sends:
        if copy is not None:
            copy.wait_send()
    down_sum(2)
    result = agg[var].astype(F32) + total[...]
    for i in (1, 2, 3):
        recv(got_z.at[i], ("rz", i))
        result = result + got_z[i].astype(F32)
    out[...] = result.astype(BF16)
    for mine, copy in optional:
        @pl.when(jnp.logical_not(mine))
        def _(copy=copy):
            copy.wait_send()
    assert len(keys) <= N_SEMS and len(sends) <= N_SEMS


def shards(pixels, w_embed, var_embed, var_mask, agg_query, ln_gain, w_up, w_down):
    vmem = pltpu.VMEM
    return pl.pallas_call(
        kernel,
        out_shape=jax.ShapeDtypeStruct((TOK, COLS), BF16),
        in_specs=[pl.BlockSpec(memory_space=pl.ANY)] * 8,
        out_specs=pl.BlockSpec(memory_space=pltpu.VMEM),
        scratch_shapes=[
            vmem((OWN_VARS, PIX, TOK), BF16),
            vmem((OWN_VARS, PIX, D), BF16),
            vmem((OWN_VARS, D), BF16),
            vmem((N_VARS,), jnp.int32),
            vmem((COLS,), BF16),
            vmem((D,), BF16),
            vmem((16, ROWS, HS), F32),
            vmem((ROWS, TOK), F32),
            vmem((4, 4, ROWS, HS), BF16),
            vmem((4, 4, ROWS, HS), BF16),
            vmem((2, 4, 4, ROWS, HS), BF16),
            vmem((4, 4, ROWS, TOK), BF16),
            vmem((16, TOK, COLS), BF16),
            vmem((4, TOK, 1024), BF16),
            vmem((4, 8, 128, FF), BF16),
            vmem((4, 4, FF, COLS), BF16),
            vmem((4, TOK, COLS), F32),
            vmem((4, 4, TOK, COLS), BF16),
            vmem((4, 4, TOK, COLS), BF16),
            vmem((4, TOK, COLS), BF16),
            vmem((TOK, FF), F32),
            vmem((TOK, COLS), F32),
            pltpu.SemaphoreType.DMA((8,)),
            pltpu.SemaphoreType.DMA((N_SEMS,)),
            pltpu.SemaphoreType.DMA((N_SEMS,)),
        ],
        compiler_params=pltpu.CompilerParams(
            collective_id=0, has_side_effects=True, vmem_limit_bytes=56 * 1024 * 1024
        ),
    )(pixels, w_embed, var_embed, var_mask, agg_query, ln_gain, w_up, w_down)


def solution(mesh):
    return jax.shard_map(
        shards,
        mesh=mesh,
        in_specs=(
            P("var", None, "seq"),
            P("var", None, None),
            P("var", None),
            P(),
            P("var"),
            P(),
            P("seq", "var"),
            P("var", "seq"),
        ),
        out_specs=P("seq", "var"),
        check_vma=False,
    )
```

time: 500 us -> 101 us (0.20)
  the two profiles are of different devices: /device:TPU:6 before, /device:TPU:64 now
where the time goes in v1:
time: 101 us
  Pallas kernels  99.7 us (99%)
  local copies, waits for them, and re-layouts  1.47 us (1%)
    pallas_call x1, Pallas kernels, shards(): pl.pallas_call(kernel, out_shape=jax.ShapeDtypeStruct((TOK, COLS), BF16),...  99.7 us

profile of v1, /device:TPU:64, one launch (start us, length us, event | category | flops | bytes accessed | tf_op | source)
XLA Modules:
  0.0 101.1 jit_solution(1446923760790103395)
XLA Ops:
  0.0 99.7 %shard_map.82 = bf16[128,256]{1,0:T(8,128)(2,1)} custom-call(bf16[6,4,128]{2,1,0:T(4,128)(2,1)} %pix_in.1, bf16[6,4,4096]{2,1,0:T(4,128)(2,1)} %emb_in.1, bf16[6,4096]{1,0:T(8,128)(2,1)} %bias_in.1, s32[96]{0:T(128)} %mask_in.1, bf16[256]{0:T(256)(128)(2,1)} %query_in.1, bf16[4096]{0:T(1024)(128)(2,1)} %gain_in.1, bf16[128,512]{1,0:T(8,128)(2,1)} %up_in.1, ...), custom_call_target="tpu_custom_call" | custom-call | tf_op jit(solution)/shard_map/pallas_call | solution.py:405
  99.7 1.5 %copy.10 = bf16[128,256]{1,0:T(8,128)(2,1)} copy(bf16[128,256]{1,0:T(8,128)(2,1)} %shard_map.82) | data formatting | bytes 131072

commit v2 on v0

v2 whole, which is shorter than its diff:
```python
import math

import jax
import jax.numpy as jnp
from jax import lax
from jax.experimental import pallas as pl
from jax.experimental.pallas import tpu as pltpu
from jax.sharding import PartitionSpec as P

MESH = pl.DeviceIdType.MESH
F32, BF16 = jnp.float32, jnp.bfloat16
PIX, HS = 4, 128
N_VARS = 96
OWN_VARS = 6
ROWS = 32
DEPTH = 16 * ROWS
TOK, COLS, D, FF = 128, 256, 4096, 512
N_SENT, N_RECV = 14, 120
SPLIT = (2, 2)
SPLIT_NEAR = (2, 2)
ORDER = (
    ("start",), ("x0", 0), ("x0", 1), ("py",), ("X", 0, 0, -1, 0), ("X", 0, 0, 1, 1), ("ty",), ("XR", 0, 0, -1),
    ("XR", 0, 0, 1), ("X", 1, 0, -1, 0), ("X", 1, 0, 1, 1), ("XR", 1, 0, -1), ("XR", 1, 0, 1), ("ts",),
    ("XR", 0, 0, 2), ("agg",), ("Z", 0, -1, 0), ("Z", 0, 1, 1), ("z1",), ("XR", 1, 0, 2), ("X", 0, -1, -1, 0),
    ("Z", 0, -1, 1), ("S", 0, -1, 0), ("Z", 0, 1, 0), ("S", 0, 1, 0), ("ayz", 1), ("X", 0, 1, 1, 1), ("ayz", 2),
    ("X", 0, -1, 1, 1), ("XR", 0, -1, 1), ("XR", 0, -1, -1), ("XR", 0, 1, 1), ("ayz", 3), ("X", 0, 1, -1, 0),
    ("XR", 0, 1, -1), ("XR", 0, -1, 2), ("XR", 0, 1, 2), ("Z", 0, 2, 0), ("Z", 0, 2, 1), ("S", 0, 2, 0), ("ln",),
    ("up", 0), ("up", -1), ("up", 1), ("X", 0, 2, -1, 0), ("XR", 0, 2, -1), ("X", 0, 2, 1, 1), ("XR", 0, 2, 1),
    ("Z", 1, -1, 0), ("Z", 1, 1, 1), ("XR", 0, 2, 2), ("X", 1, -1, -1, 0), ("up", 2), ("hid",), ("dp", 0, 0),
    ("Z", 1, -1, 1), ("S", 1, -1, 0), ("Z", 1, 1, 0), ("S", 1, 1, 0), ("dp", 0, -1), ("X", 1, 1, 1, 1), ("dp", 0, 1),
    ("dp", 0, 2), ("dp", -1, 0), ("dp", 1, 0), ("XR", 1, -1, -1), ("X", 1, -1, 1, 1), ("XR", 1, -1, 1),
    ("dp", -1, -1), ("dp", -1, 1), ("Z", 1, 2, 0), ("Z", 1, 2, 1), ("S", 1, 2, 0), ("X", 1, 1, -1, 0),
    ("XR", 1, 1, -1), ("XR", 1, 1, 1), ("ds", 0), ("dp", 2, 0), ("dp", 1, -1), ("dp", 1, 1), ("XR", 1, -1, 2),
    ("X", 1, 2, -1, 0), ("dp", -1, 2), ("XR", 1, 2, -1), ("X", 1, 2, 1, 1), ("XR", 1, 2, 1), ("dp", 2, -1),
    ("XR", 1, 1, 2), ("dp", 2, 1), ("ds", -1), ("dp", 1, 2), ("XR", 1, 2, 2), ("sent",), ("dp", 2, 2), ("ds", 1),
    ("ds", 2), ("fin",),
)


def block_of(iota):
    block, row = iota // ROWS, iota % ROWS
    owner = (block % 4) * 4 + block // 4
    local = jnp.where(row < OWN_VARS * PIX, row // PIX, row - OWN_VARS * PIX)
    return owner * OWN_VARS + local, row < OWN_VARS * (PIX + 1)


def kernel(
    pix_in, emb_in, bias_in, mask_in, query_in, gain_in, up_in, down_in, out,
    pix, emb, bias, mask, query, gain, rows_f, pix_f,
    tab_out, tab_mid, tab, pat, agg, norm, up, down, own_sum, term, got_y, got_z, summed, hidden_ref, part, total,
    local_sem, send_sem, recv_sem,
):
    var, seq = lax.axis_index("var"), lax.axis_index("seq")
    zl, y = var // 4, lax.rem(var, 4)
    zh, x, core = seq // 8, lax.rem(seq // 2, 4), lax.rem(seq, 2)
    z = zh * 4 + zl
    other = 1 - core

    def mod4(v):
        return lax.rem(v + 4, 4)

    def at_var(zl_, y_):
        return (zl_ * 4 + y_, seq)

    def at_seq(a, b, core_):
        return (var, mod4(zh + a) * 8 + mod4(x + b) * 2 + core_)

    def at_z(d):
        z_ = lax.rem(z + d + 16, 16)
        return (lax.rem(z_, 4) * 4 + y, (z_ // 4) * 8 + x * 2 + core)

    sibling = at_seq(0, 0, other)

    locals_ = []
    for i, (src, dst) in enumerate(
        (
            (pix_in, pix),
            (emb_in, emb),
            (bias_in, bias),
            (mask_in, mask),
            (query_in, query),
            (gain_in, gain),
            (up_in, up.at[zh, x, core]),
            (down_in, down.at[zh, x, :, pl.ds(pl.multiple_of(core * HS, HS), HS)]),
        )
    ):
        locals_.append(pltpu.make_async_copy(src, dst, local_sem.at[i]))
        locals_[-1].start()

    barrier = pltpu.get_barrier_semaphore()
    peers = [at_z(1), at_z(-1), at_z(2), at_z(-2), sibling]
    peers += [at_var(mod4(zl + i), y) for i in (1, 2, 3)]
    peers += [at_var(zl, mod4(y + i)) for i in (1, 2, 3)]
    peers += [at_seq(1, 0, core), at_seq(-1, 0, core), at_seq(0, 1, core), at_seq(0, -1, core)]
    for peer in peers:
        pl.semaphore_signal(barrier, inc=1, device_id=peer, device_id_type=MESH)

    groups, keys = {}, {}

    def sem_of(key):
        return keys.setdefault(key, len(keys))

    def copy_of(src, dst, group, key, device):
        return pltpu.make_async_remote_copy(
            src_ref=src,
            dst_ref=dst,
            send_sem=send_sem.at[groups.setdefault(group, len(groups))],
            recv_sem=recv_sem.at[sem_of(key)],
            device_id=device,
            device_id_type=MESH,
        )

    def send(src, dst, group, key, device):
        copy_of(src, dst, group, key, device).start()

    def recv(view, key):
        copy_of(view, view, next(iter(groups)), key, sibling).wait_recv()

    def sent(view, group):
        copy_of(view, view, group, next(iter(keys)), sibling).wait_send()

    for i in range(3):
        locals_[i].wait()
    rows_f[:, OWN_VARS * (PIX + 1) :, :] = jnp.zeros((16, ROWS - OWN_VARS * (PIX + 1), HS), F32)
    for j in range(16):
        col = pl.ds(pl.multiple_of(j * COLS + core * HS, HS), HS)
        for v in range(OWN_VARS):
            rows_f[j, v * PIX : (v + 1) * PIX, :] = emb[v, :, col].astype(F32)
        rows_f[j, OWN_VARS * PIX : OWN_VARS * (PIX + 1), :] = bias[:, col].astype(F32)
    for j in range(16):
        tab_out[j // 4, j % 4] = rows_f[j].astype(BF16)
    row = lax.broadcasted_iota(jnp.int32, (ROWS, TOK), 0)
    pix_f[...] = jnp.where(row < OWN_VARS * (PIX + 1), 1.0, 0.0)
    for v in range(OWN_VARS):
        pix_f[v * PIX : (v + 1) * PIX, :] = pix[v].astype(F32)
    pat[y, zl] = pix_f[...].astype(BF16)

    pl.semaphore_wait(barrier, len(peers))


    def pieces(m, a):
        return (SPLIT if a % 4 else SPLIT_NEAR)[m]

    def rows_of(m, a, p, count=1):
        n = (HS, FF)[m] // pieces(m, a)
        return pl.ds(p * n, n * count)

    def block(m, a, b, core_):
        if m == 0:
            return up.at[mod4(zh + a), mod4(x + b), core_]
        return down.at[mod4(zh + a), mod4(x + b), :, pl.ds(pl.multiple_of(core_ * HS, HS), HS)]

    def piece(m, a, b, p, count=1):
        if m == 0:
            return block(m, a, b, core).at[rows_of(m, a, p, count)]
        cols = pl.ds(pl.multiple_of(core * HS, HS), HS)
        return down.at[mod4(zh + a), mod4(x + b), rows_of(m, a, p, count), cols]

    def z_key(m, a, p):
        return ("z", m, a % 4, p)

    def x_key(m, a, b, p):
        n = pieces(m, a)
        alone = (b % 4 == 3 and p < n // 2) or (b % 4 == 1 and p >= n // 2)
        return ("x", m, a % 4, b % 4, p if alone else "rest")

    def z_send(m, a, p, way):
        step = {"z+": 1, "z-": -1}[way]
        if a == 0:
            rows = rows_of(m, 1, p)
            src = (up_in, down_in)[m].at[rows]
            if m == 0:
                dst = up.at[zh, x, core].at[rows]
            else:
                dst = down.at[zh, x, rows, pl.ds(pl.multiple_of(core * HS, HS), HS)]
        else:
            src = dst = piece(m, a, 0, p)
        send(src, dst, ("z", m), z_key(m, a - step, p), at_seq(step, 0, core))

    def x_send(m, a, b, p, way):
        step = {"x+": 1, "x-": -1}[way]
        src = dst = piece(m, a, b, p)
        if a == 0 and b == 0:
            src = (up_in, down_in)[m].at[rows_of(m, 0, p)]
        send(src, dst, ("x", m), x_key(m, a, b - step, p), at_seq(0, step, core))

    def s_key(m, a, b):
        return ("s", m, a % 4, b % 4 if m == 1 and a else 0)

    def swap(m, a, b):
        place = block(m, a, b, core)
        src = (up_in, down_in)[m] if a == 0 and b == 0 else place
        send(src, place, ("s", m), s_key(m, a, b), sibling)

    def z_first(m):
        n = pieces(m, 1)
        for i in range(n):
            z_send(m, 0, i, "z+")
            z_send(m, 0, n - 1 - i, "z-")

    def x_first(m):
        n = pieces(m, 0)
        for i in range(n):
            x_send(m, 0, 0, i, "x+")
            x_send(m, 0, 0, n - 1 - i, "x-")
        swap(m, 0, 0)

    def z_piece(m, a, p):
        n = pieces(m, a)
        recv(piece(m, a, 0, p), z_key(m, a, p))
        if a == -1 and p < n // 2:
            z_send(m, a, p, "z+")
        if a == 1 and p >= n // 2:
            z_send(m, a, p, "z-")
        x_send(m, a, 0, p, "x+")
        x_send(m, a, 0, p, "x-")

    def x_piece(m, a, b, p):
        recv(piece(m, a, b, p), x_key(m, a, b, p))
        x_send(m, a, b, p, "x+" if b == -1 else "x-")

    def x_rest(m, a, b):
        n = pieces(m, a)
        first, count = {-1: (n // 2, n // 2), 1: (0, n // 2), 2: (0, n)}[b]
        recv(piece(m, a, b, first, count), x_key(m, a, b, first))
        swap(m, a, b)

    def start():
        for i in (1, 2, 3):
            send(pat.at[y, zl], pat.at[y, zl], "pz", "pz", at_var(mod4(zl + i), y))
        for i, step in ((1, 1), (3, -1), (2, 2 - 4 * core)):
            send(tab_out.at[mod4(zl + i)], tab_mid.at[zl], "tz", "tz", at_z(step))
        z_first(0)
        tab_mid[zl] = tab_out[zl]

    def points_y():
        recv(pat.at[0, 0:3], "pz")
        for i in (1, 2, 3):
            send(pat.at[y], pat.at[y], "py", "py", at_var(zl, mod4(y + i)))

    def table_y():
        recv(tab_mid.at[0:3], "tz")
        for i in (1, 2, 3):
            y_ = mod4(y + i)
            send(tab_mid.at[:, y_], tab.at[core, y], "ty", "ty", at_var(zl, y_))
        tab[core, y] = tab_mid[:, y]

    def table_swap():
        recv(tab.at[core, 0:3], "ty")
        send(tab.at[core], tab.at[core], "ts", "ts", sibling)

    def aggregate():
        recv(pat.at[0:3], "py")
        recv(tab.at[other], "ts")
        locals_[3].wait()
        locals_[4].wait()
        points = pat[...].reshape(DEPTH, TOK)
        points_f = points.astype(F32)
        twice = jnp.concatenate([points_f, points_f], axis=1)
        query_f = query[...].astype(F32).reshape(1, COLS)
        tables = [tab[h].reshape(DEPTH, HS) for h in range(2)]
        shares = []
        for h in range(2):
            dots = jnp.sum(tables[h].astype(F32) * query_f[:, h * HS : (h + 1) * HS], axis=1, keepdims=True)
            shares.append((dots * (1.0 / math.sqrt(HS))) * points_f)
        share = jnp.concatenate(shares, axis=1)
        which, real = block_of(lax.broadcasted_iota(jnp.int32, (N_VARS, DEPTH), 1))
        collect = jnp.where(
            (which == lax.broadcasted_iota(jnp.int32, (N_VARS, DEPTH), 0)) & real, 1.0, 0.0
        ).astype(BF16)
        scores = jnp.zeros((N_VARS, COLS), F32)
        for _ in range(3):
            piece = share.astype(BF16)
            share = share - piece.astype(F32)
            scores = scores + jnp.dot(collect, piece, preferred_element_type=F32)
        diagonal = lax.broadcasted_iota(jnp.int32, (N_VARS, N_VARS), 0) == lax.broadcasted_iota(
            jnp.int32, (N_VARS, N_VARS), 1
        )
        keep = jnp.sum(
            jnp.where(diagonal, mask[...].astype(F32).reshape(1, N_VARS), 0.0), axis=1, keepdims=True
        )
        scores = jnp.where(keep > 0.0, scores, -1e30)
        expo = jnp.exp(scores - jnp.max(scores, axis=0, keepdims=True))
        weights = (expo / jnp.sum(expo, axis=0, keepdims=True)).astype(BF16)
        which, real = block_of(lax.broadcasted_iota(jnp.int32, (DEPTH, N_VARS), 0))
        expand = jnp.where(
            (which == lax.broadcasted_iota(jnp.int32, (DEPTH, N_VARS), 1)) & real, 1.0, 0.0
        ).astype(BF16)
        mixed = jnp.dot(expand, weights, preferred_element_type=F32) * twice
        high = mixed.astype(BF16)
        low = (mixed - high.astype(F32)).astype(BF16)
        over_rows = (((0,), (0,)), ((), ()))
        merged = []
        for h in range(2):
            cols = slice(h * HS, (h + 1) * HS)
            merged.append(
                lax.dot_general(high[:, cols], tables[h], over_rows, preferred_element_type=F32)
                + lax.dot_general(low[:, cols], tables[h], over_rows, preferred_element_type=F32)
            )
        agg[var] = jnp.concatenate(merged, axis=1).astype(BF16)

        for i in (1, 2, 3):
            send(agg.at[var], agg.at[var], "agg", ("az", i), at_var(mod4(zl + i), y))
        for i in (1, 3, 2):
            send(agg.at[var], agg.at[var], "agg", "ay", at_var(zl, mod4(y + i)))

    def features_y(j):
        place = agg.at[mod4(zl - j) * 4 + y]
        recv(place, ("az", j))
        for i in (1, 3, 2):
            send(place, place, "agg", "ay", at_var(zl, mod4(y + i)))

    def layer_norm():
        recv(agg.at[0:12], "ay")
        sums = jnp.zeros((TOK, COLS), F32)
        for v in range(16):
            sums = sums + agg[v].astype(F32)
        mean = jnp.sum(sums, axis=1, keepdims=True) * (1.0 / D)
        sums = jnp.zeros((TOK, COLS), F32)
        for v in range(16):
            centered = agg[v].astype(F32) - mean
            sums = sums + centered * centered
        variance = jnp.sum(sums, axis=1, keepdims=True) * (1.0 / D)
        scale = lax.rsqrt(variance + 1e-05)
        locals_[5].wait()
        for v in range(16):
            cols = slice(v * COLS, (v + 1) * COLS)
            gains = gain[cols].astype(F32).reshape(1, COLS)
            norm[v // 4, :, (v % 4) * COLS : (v % 4 + 1) * COLS] = (
                (agg[v].astype(F32) - mean) * scale * gains
            ).astype(BF16)

    def up_part(a):
        if a == 0:
            locals_[6].wait()
        q = mod4(zh + a)
        recv(up.at[q, :, other], s_key(0, a, 0))
        value = jnp.dot(norm[q], up[q].reshape(1024, FF), preferred_element_type=F32)
        part[...] = value if a == 0 else part[...] + value

    def activate():
        hidden_ref[...] = jax.nn.gelu(part[...], approximate=True).astype(BF16)

    def down_part(a, b):
        if a == 0 and b == 0:
            locals_[7].wait()
        q, y_ = mod4(zh + a), mod4(x + b)
        cols = pl.ds(pl.multiple_of(other * HS, HS), HS)
        if a:
            recv(down.at[q, y_, :, cols], s_key(1, a, b))
        elif b == 0:
            recv(down.at[q, :, :, cols], s_key(1, a, b))
        value = jnp.dot(hidden_ref[...], down[q, y_], preferred_element_type=F32)
        away = mod4(y_ - y)

        @pl.when(away == 0)
        def _():
            own_sum[a % 4] = value

        term[a % 4, b % 4] = value.astype(BF16)

        @pl.when(away != 0)
        def _():
            send(term.at[a % 4, b % 4], got_y.at[a % 4, away], "ry", ("ry", a % 4), at_var(zl, y_))

    def down_sum(a):
        a = a % 4
        q = mod4(zh + a)
        recv(got_y.at[a, 1:4], ("ry", a))
        value = own_sum[a]
        for i in (1, 2, 3):
            value = value + got_y[a, i].astype(F32)
        away = mod4(zl - q)

        @pl.when(away == 0)
        def _():
            total[...] = value

        summed[a] = value.astype(BF16)

        @pl.when(away != 0)
        def _():
            send(summed.at[a], got_z.at[away], "rz", "rz", at_var(q, y))

    def all_sent():
        for m in (0, 1):
            sent(up.at[0, 0:3, 0], ("z", m))
            sent(up.at[0:3, :, 0], ("x", m))
            sent(up.at[0:2], ("s", m))
        sent(pat.at[0, 0:3], "pz")
        sent(pat.at[0:3], "py")
        sent(tab_mid.at[0:3], "tz")
        sent(tab_mid.at[0:3], "ty")
        sent(tab.at[0], "ts")
        sent(agg.at[0:15], "agg")

    def finish():
        result = agg[var].astype(F32) + total[...]
        recv(got_z.at[1:4], "rz")
        for i in (1, 2, 3):
            result = result + got_z[i].astype(F32)
        out[...] = result.astype(BF16)
        sent(got_y.at[0:3], "ry")
        sent(got_z.at[0:3], "rz")

    steps = {
        "start": start,
        "x0": x_first,
        "z1": lambda: z_first(1),
        "Z": z_piece,
        "X": x_piece,
        "XR": x_rest,
        "S": swap,
        "py": points_y,
        "ty": table_y,
        "ts": table_swap,
        "agg": aggregate,
        "ayz": features_y,
        "ln": layer_norm,
        "up": up_part,
        "hid": activate,
        "dp": down_part,
        "sent": all_sent,
        "ds": down_sum,
        "fin": finish,
    }
    for name, *rest in ORDER:
        steps[name](*rest)
    assert len(keys) <= N_RECV and len(groups) <= N_SENT


def shards(pixels, w_embed, var_embed, var_mask, agg_query, ln_gain, w_up, w_down):
    vmem = pltpu.VMEM
    return pl.pallas_call(
        kernel,
        out_shape=jax.ShapeDtypeStruct((TOK, COLS), BF16),
        in_specs=[pl.BlockSpec(memory_space=pl.ANY)] * 8,
        out_specs=pl.BlockSpec(memory_space=pltpu.VMEM),
        scratch_shapes=[
            vmem((OWN_VARS, PIX, TOK), BF16),
            vmem((OWN_VARS, PIX, D), BF16),
            vmem((OWN_VARS, D), BF16),
            vmem((N_VARS,), jnp.int32),
            vmem((COLS,), BF16),
            vmem((D,), BF16),
            vmem((16, ROWS, HS), F32),
            vmem((ROWS, TOK), F32),
            vmem((4, 4, ROWS, HS), BF16),
            vmem((4, 4, ROWS, HS), BF16),
            vmem((2, 4, 4, ROWS, HS), BF16),
            vmem((4, 4, ROWS, TOK), BF16),
            vmem((16, TOK, COLS), BF16),
            vmem((4, TOK, 1024), BF16),
            vmem((4, 4, 2, 128, FF), BF16),
            vmem((4, 4, FF, COLS), BF16),
            vmem((4, TOK, COLS), F32),
            vmem((4, 4, TOK, COLS), BF16),
            vmem((4, 4, TOK, COLS), BF16),
            vmem((4, TOK, COLS), BF16),
            vmem((4, TOK, COLS), BF16),
            vmem((TOK, FF), BF16),
            vmem((TOK, FF), F32),
            vmem((TOK, COLS), F32),
            pltpu.SemaphoreType.DMA((8,)),
            pltpu.SemaphoreType.DMA((N_SENT,)),
            pltpu.SemaphoreType.DMA((N_RECV,)),
        ],
        compiler_params=pltpu.CompilerParams(
            collective_id=0, has_side_effects=True, vmem_limit_bytes=56 * 1024 * 1024
        ),
    )(pixels, w_embed, var_embed, var_mask, agg_query, ln_gain, w_up, w_down)


def solution(mesh):
    return jax.shard_map(
        shards,
        mesh=mesh,
        in_specs=(
            P("var", None, "seq"),
            P("var", None, None),
            P("var", None),
            P(),
            P("var"),
            P(),
            P("seq", "var"),
            P("var", "seq"),
        ),
        out_specs=P("seq", "var"),
        check_vma=False,
    )
```

time: 500 us -> 87.2 us (0.17)
  the two profiles are of different devices: /device:TPU:6 before, /device:TPU:58 now
where the time goes in v2:
time: 87.2 us; the launch traced here: 87 us
  Pallas kernels  85.5 us (98%)
  local copies, waits for them, and re-layouts  1.47 us (2%)
    pallas_call x1, Pallas kernels, shards(): pl.pallas_call(kernel, out_shape=jax.ShapeDtypeStruct((TOK, COLS), BF16),...  85.5 us

profile of v2, /device:TPU:58, one launch (start us, length us, event | category | flops | bytes accessed | tf_op | source)
XLA Modules:
  0.0 87.0 jit_solution(961092758049196084)
XLA Ops:
  0.0 85.5 %shard_map.82 = bf16[128,256]{1,0:T(8,128)(2,1)} custom-call(bf16[6,4,128]{2,1,0:T(4,128)(2,1)} %pix_in.1, bf16[6,4,4096]{2,1,0:T(4,128)(2,1)} %emb_in.1, bf16[6,4096]{1,0:T(8,128)(2,1)} %bias_in.1, s32[96]{0:T(128)} %mask_in.1, bf16[256]{0:T(256)(128)(2,1)} %query_in.1, bf16[4096]{0:T(1024)(128)(2,1)} %gain_in.1, bf16[128,512]{1,0:T(8,128)(2,1)} %up_in.1, ...), custom_call_target="tpu_custom_call" | custom-call | tf_op jit(solution)/shard_map/pallas_call | solution.py:434
  85.5 1.5 %copy.10 = bf16[128,256]{1,0:T(8,128)(2,1)} copy(bf16[128,256]{1,0:T(8,128)(2,1)} %shard_map.82) | data formatting | bytes 131072

commit v3 on v2

--- a/solution.py
+++ b/solution.py
@@ -16,24 +16,26 @@
 DEPTH = 16 * ROWS
 TOK, COLS, D, FF = 128, 256, 4096, 512
 N_SENT, N_RECV = 14, 120
-SPLIT = (2, 2)
+SPLIT = (2, 4)
 SPLIT_NEAR = (2, 2)
 ORDER = (
-    ("start",), ("x0", 0), ("x0", 1), ("py",), ("X", 0, 0, -1, 0), ("X", 0, 0, 1, 1), ("ty",), ("XR", 0, 0, -1),
-    ("XR", 0, 0, 1), ("X", 1, 0, -1, 0), ("X", 1, 0, 1, 1), ("XR", 1, 0, -1), ("XR", 1, 0, 1), ("ts",),
-    ("XR", 0, 0, 2), ("agg",), ("Z", 0, -1, 0), ("Z", 0, 1, 1), ("z1",), ("XR", 1, 0, 2), ("X", 0, -1, -1, 0),
-    ("Z", 0, -1, 1), ("S", 0, -1, 0), ("Z", 0, 1, 0), ("S", 0, 1, 0), ("ayz", 1), ("X", 0, 1, 1, 1), ("ayz", 2),
-    ("X", 0, -1, 1, 1), ("XR", 0, -1, 1), ("XR", 0, -1, -1), ("XR", 0, 1, 1), ("ayz", 3), ("X", 0, 1, -1, 0),
-    ("XR", 0, 1, -1), ("XR", 0, -1, 2), ("XR", 0, 1, 2), ("Z", 0, 2, 0), ("Z", 0, 2, 1), ("S", 0, 2, 0), ("ln",),
-    ("up", 0), ("up", -1), ("up", 1), ("X", 0, 2, -1, 0), ("XR", 0, 2, -1), ("X", 0, 2, 1, 1), ("XR", 0, 2, 1),
-    ("Z", 1, -1, 0), ("Z", 1, 1, 1), ("XR", 0, 2, 2), ("X", 1, -1, -1, 0), ("up", 2), ("hid",), ("dp", 0, 0),
-    ("Z", 1, -1, 1), ("S", 1, -1, 0), ("Z", 1, 1, 0), ("S", 1, 1, 0), ("dp", 0, -1), ("X", 1, 1, 1, 1), ("dp", 0, 1),
-    ("dp", 0, 2), ("dp", -1, 0), ("dp", 1, 0), ("XR", 1, -1, -1), ("X", 1, -1, 1, 1), ("XR", 1, -1, 1),
-    ("dp", -1, -1), ("dp", -1, 1), ("Z", 1, 2, 0), ("Z", 1, 2, 1), ("S", 1, 2, 0), ("X", 1, 1, -1, 0),
-    ("XR", 1, 1, -1), ("XR", 1, 1, 1), ("ds", 0), ("dp", 2, 0), ("dp", 1, -1), ("dp", 1, 1), ("XR", 1, -1, 2),
-    ("X", 1, 2, -1, 0), ("dp", -1, 2), ("XR", 1, 2, -1), ("X", 1, 2, 1, 1), ("XR", 1, 2, 1), ("dp", 2, -1),
-    ("XR", 1, 1, 2), ("dp", 2, 1), ("ds", -1), ("dp", 1, 2), ("XR", 1, 2, 2), ("sent",), ("dp", 2, 2), ("ds", 1),
-    ("ds", 2), ("fin",),
+    ("x0", 0), ("z0", 0), ("pack",), ("start",), ("X", 0, 0, 1, 1), ("x0", 1), ("X", 0, 0, -1, 0), ("X", 1, 0, -1, 0),
+    ("z0", 1), ("X", 1, 0, 1, 1), ("Z", 0, 1, 1), ("py",), ("Z", 0, -1, 0), ("ty",), ("z1", 1), ("ts",),
+    ("XR", 0, 0, 2), ("Z", 0, -1, 1), ("agg",), ("Z", 0, 1, 0), ("X", 0, -1, 1, 1), ("z1", 2), ("XR", 0, -1, 1),
+    ("X", 0, 1, 1, 1), ("S", 0, -1, 0), ("X", 0, -1, -1, 0), ("XR", 0, -1, 2), ("z1", 0), ("X", 0, 1, -1, 0),
+    ("Z2", 0, 0), ("z1", 3), ("XR", 0, 0, -1), ("ayz", 1), ("XR", 0, 1, -1), ("ayz", 2), ("X", 0, 2, 1, 1),
+    ("X", 0, 2, -1, 0), ("ayz", 3), ("Z", 1, 1, 2), ("Z", 1, -1, 2), ("Z", 1, -1, 1), ("XR", 0, 2, -1),
+    ("XR", 0, 2, 1), ("Z", 1, 1, 1), ("XR", 0, 1, 2), ("S", 0, 1, 0), ("XR", 0, -1, -1), ("Z", 1, -1, 0),
+    ("XR", 0, 0, 1), ("S", 0, 2, 0), ("Z", 1, -1, 3), ("Z", 1, 1, 3), ("XR", 1, 0, -1), ("Z", 1, 1, 0),
+    ("X", 1, 1, 1, 2), ("XR", 0, 1, 1), ("XR", 0, 2, 2), ("X", 1, -1, -1, 1), ("XR", 1, 0, 2), ("ln",),
+    ("X", 1, -1, 1, 2), ("up", 0), ("XR", 1, 0, 1), ("up", 1), ("up", -1), ("up", 2), ("S", 1, 1, 0),
+    ("X", 1, -1, -1, 0), ("hid",), ("dp", 0, 0), ("XR", 1, -1, -1), ("X", 1, -1, 1, 3), ("S", 1, -1, 0),
+    ("X", 1, 1, 1, 3), ("X", 1, 1, -1, 0), ("XR", 1, -1, 1), ("dp", 0, -1), ("XR", 1, 1, 1), ("Z2", 1, 1),
+    ("dp", 1, 0), ("X", 1, 1, -1, 1), ("dp", 0, 2), ("dp", 0, 1), ("dp", -1, -1), ("dp", -1, 0), ("Z2", 1, 0),
+    ("XR", 1, -1, 2), ("dp", -1, 1), ("X", 1, 2, -1, 1), ("X", 1, 2, 1, 2), ("XR", 1, 1, -1), ("dp", -1, 2),
+    ("dp", 1, -1), ("XR", 1, 1, 2), ("dp", 1, 1), ("S", 1, 2, 0), ("X", 1, 2, -1, 0), ("X", 1, 2, 1, 3), ("dp", 1, 2),
+    ("XR", 1, 2, 1), ("XR", 1, 2, -1), ("dp", 2, 0), ("ds", 0), ("dp", 2, 1), ("dp", 2, -1), ("XR", 1, 2, 2),
+    ("ds", -1), ("dp", 2, 2), ("ds", 1), ("sent",), ("ds", 2), ("fin",),
 )
 
 
@@ -119,22 +121,6 @@
     def sent(view, group):
         copy_of(view, view, group, next(iter(keys)), sibling).wait_send()
 
-    for i in range(3):
-        locals_[i].wait()
-    rows_f[:, OWN_VARS * (PIX + 1) :, :] = jnp.zeros((16, ROWS - OWN_VARS * (PIX + 1), HS), F32)
-    for j in range(16):
-        col = pl.ds(pl.multiple_of(j * COLS + core * HS, HS), HS)
-        for v in range(OWN_VARS):
-            rows_f[j, v * PIX : (v + 1) * PIX, :] = emb[v, :, col].astype(F32)
-        rows_f[j, OWN_VARS * PIX : OWN_VARS * (PIX + 1), :] = bias[:, col].astype(F32)
-    for j in range(16):
-        tab_out[j // 4, j % 4] = rows_f[j].astype(BF16)
-    row = lax.broadcasted_iota(jnp.int32, (ROWS, TOK), 0)
-    pix_f[...] = jnp.where(row < OWN_VARS * (PIX + 1), 1.0, 0.0)
-    for v in range(OWN_VARS):
-        pix_f[v * PIX : (v + 1) * PIX, :] = pix[v].astype(F32)
-    pat[y, zl] = pix_f[...].astype(BF16)
-
     pl.semaphore_wait(barrier, len(peers))
 
 
@@ -192,11 +178,9 @@
         src = (up_in, down_in)[m] if a == 0 and b == 0 else place
         send(src, place, ("s", m), s_key(m, a, b), sibling)
 
-    def z_first(m):
-        n = pieces(m, 1)
-        for i in range(n):
-            z_send(m, 0, i, "z+")
-            z_send(m, 0, n - 1 - i, "z-")
+    def z_first(m, i):
+        z_send(m, 0, i, "z+")
+        z_send(m, 0, pieces(m, 1) - 1 - i, "z-")
 
     def x_first(m):
         n = pieces(m, 0)
@@ -215,6 +199,15 @@
         x_send(m, a, 0, p, "x+")
         x_send(m, a, 0, p, "x-")
 
+    def z_far(m, low):
+        high = pieces(m, 2) - 1 - low
+        for p in (low, high):
+            recv(piece(m, 2, 0, p), z_key(m, 2, p))
+        x_send(m, 2, 0, low, "x+")
+        x_send(m, 2, 0, high, "x-")
+        x_send(m, 2, 0, high, "x+")
+        x_send(m, 2, 0, low, "x-")
+
     def x_piece(m, a, b, p):
         recv(piece(m, a, b, p), x_key(m, a, b, p))
         x_send(m, a, b, p, "x+" if b == -1 else "x-")
@@ -225,13 +218,29 @@
         recv(piece(m, a, b, first, count), x_key(m, a, b, first))
         swap(m, a, b)
 
+    def pack():
+        for i in range(3):
+            locals_[i].wait()
+        rows_f[:, OWN_VARS * (PIX + 1) :, :] = jnp.zeros((16, ROWS - OWN_VARS * (PIX + 1), HS), F32)
+        for j in range(16):
+            col = pl.ds(pl.multiple_of(j * COLS + core * HS, HS), HS)
+            for v in range(OWN_VARS):
+                rows_f[j, v * PIX : (v + 1) * PIX, :] = emb[v, :, col].astype(F32)
+            rows_f[j, OWN_VARS * PIX : OWN_VARS * (PIX + 1), :] = bias[:, col].astype(F32)
+        for j in range(16):
+            tab_out[j // 4, j % 4] = rows_f[j].astype(BF16)
+        row = lax.broadcasted_iota(jnp.int32, (ROWS, TOK), 0)
+        pix_f[...] = jnp.where(row < OWN_VARS * (PIX + 1), 1.0, 0.0)
+        for v in range(OWN_VARS):
+            pix_f[v * PIX : (v + 1) * PIX, :] = pix[v].astype(F32)
+        pat[y, zl] = pix_f[...].astype(BF16)
+        tab_mid[zl] = tab_out[zl]
+
     def start():
         for i in (1, 2, 3):
             send(pat.at[y, zl], pat.at[y, zl], "pz", "pz", at_var(mod4(zl + i), y))
         for i, step in ((1, 1), (3, -1), (2, 2 - 4 * core)):
             send(tab_out.at[mod4(zl + i)], tab_mid.at[zl], "tz", "tz", at_z(step))
-        z_first(0)
-        tab_mid[zl] = tab_out[zl]
 
     def points_y():
         recv(pat.at[0, 0:3], "pz")
@@ -404,10 +413,13 @@
         sent(got_z.at[0:3], "rz")
 
     steps = {
+        "pack": pack,
         "start": start,
+        "z0": lambda i: z_first(0, i),
         "x0": x_first,
-        "z1": lambda: z_first(1),
+        "z1": lambda i: z_first(1, i),
         "Z": z_piece,
+        "Z2": z_far,
         "X": x_piece,
         "XR": x_rest,
         "S": swap,

time: 87.2 us -> 81.6 us (0.936)
  the two profiles are of different devices: /device:TPU:58 before, /device:TPU:80 now
where the time goes in v3:
time: 81.6 us; the launch traced here: 81.5 us
  Pallas kernels  80 us (98%)
  local copies, waits for them, and re-layouts  1.47 us (2%)
    pallas_call x1, Pallas kernels, shards(): pl.pallas_call(kernel, out_shape=jax.ShapeDtypeStruct((TOK, COLS), BF16),...  80 us

profile of v3, /device:TPU:80, one launch (start us, length us, event | category | flops | bytes accessed | tf_op | source)
XLA Modules:
  0.0 81.5 jit_solution(7661099856130348092)
XLA Ops:
  0.0 80.0 %shard_map.82 = bf16[128,256]{1,0:T(8,128)(2,1)} custom-call(bf16[6,4,128]{2,1,0:T(4,128)(2,1)} %pix_in.1, bf16[6,4,4096]{2,1,0:T(4,128)(2,1)} %emb_in.1, bf16[6,4096]{1,0:T(8,128)(2,1)} %bias_in.1, s32[96]{0:T(128)} %mask_in.1, bf16[256]{0:T(256)(128)(2,1)} %query_in.1, bf16[4096]{0:T(1024)(128)(2,1)} %gain_in.1, bf16[128,512]{1,0:T(8,128)(2,1)} %up_in.1, ...), custom_call_target="tpu_custom_call" | custom-call | tf_op jit(solution)/shard_map/pallas_call | solution.py:446
  80.0 1.5 %copy.10 = bf16[128,256]{1,0:T(8,128)(2,1)} copy(bf16[128,256]{1,0:T(8,128)(2,1)} %shard_map.82) | data formatting | bytes 131072

commit v4 on v3

--- a/solution.py
+++ b/solution.py
@@ -15,33 +15,32 @@
 ROWS = 32
 DEPTH = 16 * ROWS
 TOK, COLS, D, FF = 128, 256, 4096, 512
-N_SENT, N_RECV = 14, 120
+N_SENT, N_RECV = 15, 120
 SPLIT = (2, 4)
 SPLIT_NEAR = (2, 2)
 ORDER = (
-    ("x0", 0), ("z0", 0), ("pack",), ("start",), ("X", 0, 0, 1, 1), ("x0", 1), ("X", 0, 0, -1, 0), ("X", 1, 0, -1, 0),
-    ("z0", 1), ("X", 1, 0, 1, 1), ("Z", 0, 1, 1), ("py",), ("Z", 0, -1, 0), ("ty",), ("z1", 1), ("ts",),
-    ("XR", 0, 0, 2), ("Z", 0, -1, 1), ("agg",), ("Z", 0, 1, 0), ("X", 0, -1, 1, 1), ("z1", 2), ("XR", 0, -1, 1),
-    ("X", 0, 1, 1, 1), ("S", 0, -1, 0), ("X", 0, -1, -1, 0), ("XR", 0, -1, 2), ("z1", 0), ("X", 0, 1, -1, 0),
-    ("Z2", 0, 0), ("z1", 3), ("XR", 0, 0, -1), ("ayz", 1), ("XR", 0, 1, -1), ("ayz", 2), ("X", 0, 2, 1, 1),
-    ("X", 0, 2, -1, 0), ("ayz", 3), ("Z", 1, 1, 2), ("Z", 1, -1, 2), ("Z", 1, -1, 1), ("XR", 0, 2, -1),
-    ("XR", 0, 2, 1), ("Z", 1, 1, 1), ("XR", 0, 1, 2), ("S", 0, 1, 0), ("XR", 0, -1, -1), ("Z", 1, -1, 0),
-    ("XR", 0, 0, 1), ("S", 0, 2, 0), ("Z", 1, -1, 3), ("Z", 1, 1, 3), ("XR", 1, 0, -1), ("Z", 1, 1, 0),
-    ("X", 1, 1, 1, 2), ("XR", 0, 1, 1), ("XR", 0, 2, 2), ("X", 1, -1, -1, 1), ("XR", 1, 0, 2), ("ln",),
-    ("X", 1, -1, 1, 2), ("up", 0), ("XR", 1, 0, 1), ("up", 1), ("up", -1), ("up", 2), ("S", 1, 1, 0),
-    ("X", 1, -1, -1, 0), ("hid",), ("dp", 0, 0), ("XR", 1, -1, -1), ("X", 1, -1, 1, 3), ("S", 1, -1, 0),
-    ("X", 1, 1, 1, 3), ("X", 1, 1, -1, 0), ("XR", 1, -1, 1), ("dp", 0, -1), ("XR", 1, 1, 1), ("Z2", 1, 1),
-    ("dp", 1, 0), ("X", 1, 1, -1, 1), ("dp", 0, 2), ("dp", 0, 1), ("dp", -1, -1), ("dp", -1, 0), ("Z2", 1, 0),
-    ("XR", 1, -1, 2), ("dp", -1, 1), ("X", 1, 2, -1, 1), ("X", 1, 2, 1, 2), ("XR", 1, 1, -1), ("dp", -1, 2),
-    ("dp", 1, -1), ("XR", 1, 1, 2), ("dp", 1, 1), ("S", 1, 2, 0), ("X", 1, 2, -1, 0), ("X", 1, 2, 1, 3), ("dp", 1, 2),
-    ("XR", 1, 2, 1), ("XR", 1, 2, -1), ("dp", 2, 0), ("ds", 0), ("dp", 2, 1), ("dp", 2, -1), ("XR", 1, 2, 2),
-    ("ds", -1), ("dp", 2, 2), ("ds", 1), ("sent",), ("ds", 2), ("fin",),
+    ("pack",), ("start",), ("z0", 0), ("z0", 1), ("x0", 0), ("x0", 1), ("X", 0, 0, -1, 0), ("X", 0, 0, 1, 1),
+    ("XR", 0, 0, -1), ("XR", 0, 0, 1), ("py",), ("X", 1, 0, -1, 0), ("X", 1, 0, 1, 1), ("tz",), ("XR", 1, 0, -1),
+    ("XR", 1, 0, 1), ("XR", 0, 0, 2), ("XR", 1, 0, 2), ("Z", 0, -1, 0), ("Z", 0, 1, 1), ("z1", 0), ("z1", 1),
+    ("z1", 2), ("z1", 3), ("tx",), ("X", 0, -1, -1, 0), ("agg", 0), ("Z", 0, -1, 1), ("S", 0, -1, 0), ("Z", 0, 1, 0),
+    ("S", 0, 1, 0), ("X", 0, 1, 1, 1), ("tsib", -1), ("tsib", 1), ("Z2", 0, 0), ("S", 0, 2, 0), ("agg", -1),
+    ("agg", 1), ("Z", 1, -1, 0), ("X", 0, -1, 1, 1), ("XR", 0, -1, 1), ("Z", 1, 1, 3), ("tsib", 2), ("XR", 0, -1, -1),
+    ("XR", 0, 1, 1), ("agg", 2), ("X", 0, 1, -1, 0), ("XR", 0, 1, -1), ("Z", 1, -1, 1), ("Z", 1, 1, 2),
+    ("X", 0, 2, -1, 0), ("X", 0, 2, 1, 1), ("Z", 1, -1, 2), ("Z", 1, 1, 1), ("XR", 0, 2, -1), ("XR", 0, 2, 1),
+    ("X", 1, -1, -1, 0), ("XR", 0, -1, 2), ("Z", 1, -1, 3), ("S", 1, -1, 0), ("Z", 1, 1, 0), ("XR", 0, 1, 2),
+    ("S", 1, 1, 0), ("X", 1, 1, 1, 3), ("X", 1, -1, -1, 1), ("ln",), ("Z2", 1, 0), ("XR", 0, 2, 2), ("X", 1, 1, 1, 2),
+    ("up", 0), ("X", 1, -1, 1, 2), ("up", -1), ("X", 1, 1, -1, 1), ("up", 1), ("X", 1, -1, 1, 3), ("XR", 1, -1, 1),
+    ("Z2", 1, 1), ("S", 1, 2, 0), ("XR", 1, -1, -1), ("XR", 1, 1, 1), ("up", 2), ("X", 1, 1, -1, 0), ("XR", 1, 1, -1),
+    ("hid",), ("dp", 0, 0), ("X", 1, 2, 1, 3), ("dp", 0, -1), ("dp", 0, 1), ("X", 1, 2, -1, 0), ("dp", 0, 2),
+    ("dp", -1, 0), ("dp", -1, -1), ("dp", -1, 1), ("dp", 1, 0), ("dp", 1, -1), ("dp", 1, 1), ("dp", 2, 0),
+    ("X", 1, 2, -1, 1), ("XR", 1, -1, 2), ("XR", 1, 2, -1), ("X", 1, 2, 1, 2), ("dp", -1, 2), ("XR", 1, 1, 2),
+    ("XR", 1, 2, 1), ("dp", 2, -1), ("dp", 1, 2), ("dp", 2, 1), ("XR", 1, 2, 2), ("ds", 0), ("dp", 2, 2), ("ds", -1),
+    ("ds", 1), ("ds", 2, 0), ("sent",), ("ds", 2, 1), ("fin",),
 )
 
 
 def block_of(iota):
-    block, row = iota // ROWS, iota % ROWS
-    owner = (block % 4) * 4 + block // 4
+    owner, row = iota // ROWS, iota % ROWS
     local = jnp.where(row < OWN_VARS * PIX, row // PIX, row - OWN_VARS * PIX)
     return owner * OWN_VARS + local, row < OWN_VARS * (PIX + 1)
 
@@ -49,7 +48,7 @@
 def kernel(
     pix_in, emb_in, bias_in, mask_in, query_in, gain_in, up_in, down_in, out,
     pix, emb, bias, mask, query, gain, rows_f, pix_f,
-    tab_out, tab_mid, tab, pat, agg, norm, up, down, own_sum, term, got_y, got_z, summed, hidden_ref, part, total,
+    tab_out, tab_mid, tab, collect, expand, pat, agg, norm, up, down, own_sum, term, got_y, got_z, summed, hidden_ref, part, total,
     local_sem, send_sem, recv_sem,
 ):
     var, seq = lax.axis_index("var"), lax.axis_index("seq")
@@ -93,7 +92,8 @@
     peers = [at_z(1), at_z(-1), at_z(2), at_z(-2), sibling]
     peers += [at_var(mod4(zl + i), y) for i in (1, 2, 3)]
     peers += [at_var(zl, mod4(y + i)) for i in (1, 2, 3)]
-    peers += [at_seq(1, 0, core), at_seq(-1, 0, core), at_seq(0, 1, core), at_seq(0, -1, core)]
+    peers += [at_seq(1, 0, core), at_seq(-1, 0, core)]
+    peers += [at_seq(0, i, core) for i in (1, 2, 3)]
     for peer in peers:
         pl.semaphore_signal(barrier, inc=1, device_id=peer, device_id_type=MESH)
 
@@ -219,7 +219,7 @@
         swap(m, a, b)
 
     def pack():
-        for i in range(3):
+        for i in (0, 1, 2, 4):
             locals_[i].wait()
         rows_f[:, OWN_VARS * (PIX + 1) :, :] = jnp.zeros((16, ROWS - OWN_VARS * (PIX + 1), HS), F32)
         for j in range(16):
@@ -228,60 +228,70 @@
                 rows_f[j, v * PIX : (v + 1) * PIX, :] = emb[v, :, col].astype(F32)
             rows_f[j, OWN_VARS * PIX : OWN_VARS * (PIX + 1), :] = bias[:, col].astype(F32)
         for j in range(16):
-            tab_out[j // 4, j % 4] = rows_f[j].astype(BF16)
+            tab_out[j % 4, j // 4] = rows_f[j].astype(BF16)
         row = lax.broadcasted_iota(jnp.int32, (ROWS, TOK), 0)
         pix_f[...] = jnp.where(row < OWN_VARS * (PIX + 1), 1.0, 0.0)
         for v in range(OWN_VARS):
             pix_f[v * PIX : (v + 1) * PIX, :] = pix[v].astype(F32)
-        pat[y, zl] = pix_f[...].astype(BF16)
-        tab_mid[zl] = tab_out[zl]
+        for h in range(2):
+            pix_f[ROWS - 2 + h : ROWS - 1 + h, :] = query[h * HS : (h + 1) * HS].astype(F32).reshape(1, HS)
+        pat[zl, y] = pix_f[...].astype(BF16)
+        tab_mid[y] = tab_out[y]
 
     def start():
         for i in (1, 2, 3):
-            send(pat.at[y, zl], pat.at[y, zl], "pz", "pz", at_var(mod4(zl + i), y))
-        for i, step in ((1, 1), (3, -1), (2, 2 - 4 * core)):
-            send(tab_out.at[mod4(zl + i)], tab_mid.at[zl], "tz", "tz", at_z(step))
+            send(pat.at[zl, y], pat.at[zl, y], "pz", "pz", at_var(mod4(zl + i), y))
+        for i in (1, 3, 2):
+            y_ = mod4(y + i)
+            send(tab_out.at[y_], tab_mid.at[y], "ty", "ty", at_var(zl, y_))
 
     def points_y():
-        recv(pat.at[0, 0:3], "pz")
-        for i in (1, 2, 3):
-            send(pat.at[y], pat.at[y], "py", "py", at_var(zl, mod4(y + i)))
-
-    def table_y():
-        recv(tab_mid.at[0:3], "tz")
-        for i in (1, 2, 3):
-            y_ = mod4(y + i)
-            send(tab_mid.at[:, y_], tab.at[core, y], "ty", "ty", at_var(zl, y_))
-        tab[core, y] = tab_mid[:, y]
-
-    def table_swap():
-        recv(tab.at[core, 0:3], "ty")
-        send(tab.at[core], tab.at[core], "ts", "ts", sibling)
-
-    def aggregate():
-        recv(pat.at[0:3], "py")
-        recv(tab.at[other], "ts")
-        locals_[3].wait()
-        locals_[4].wait()
-        points = pat[...].reshape(DEPTH, TOK)
-        points_f = points.astype(F32)
+        recv(pat.at[0:3, 0], "pz")
+        for i in (1, 3, 2):
+            send(pat.at[:, y], pat.at[:, y], "py", "py", at_var(zl, mod4(y + i)))
+
+    def table_z():
+        recv(tab_mid.at[0:3], "ty")
+        for step in (1, -1, 2 - 4 * core):
+            send(tab_mid.at[:, x], tab.at[core, x, zl], "tz", "tz", at_z(step))
+        tab[core, x, zl] = tab_mid[:, x]
+
+    def table_x():
+        recv(tab.at[core, x, 0:3], "tz")
+        for b in (1, -1, 2):
+            send(tab.at[core, x], tab.at[core, x], "tx", ("tx", -b % 4), at_seq(0, b, core))
+        send(tab.at[core, x], tab.at[core, x], "ts", ("ts", 0), sibling)
+
+    def table_swap(b):
+        place = tab.at[core, mod4(x + b)]
+        recv(place, ("tx", b % 4))
+        send(place, place, "ts", ("ts", b % 4), sibling)
+
+    def aggregate(b):
+        quarter = mod4(x + b)
+        if b == 0:
+            recv(pat.at[0:3], "py")
+            locals_[3].wait()
+            for ref, dim in ((collect, 1), (expand, 0)):
+                which, real = block_of(lax.broadcasted_iota(jnp.int32, ref.shape, dim))
+                own = (which == lax.broadcasted_iota(jnp.int32, ref.shape, 1 - dim)) & real
+                ref[...] = jnp.where(own, 1.0, 0.0).astype(BF16)
+        recv(tab.at[other, quarter], ("ts", b % 4))
+        points_f = pat[...].reshape(DEPTH, TOK).astype(F32)
         twice = jnp.concatenate([points_f, points_f], axis=1)
-        query_f = query[...].astype(F32).reshape(1, COLS)
-        tables = [tab[h].reshape(DEPTH, HS) for h in range(2)]
+        tables = [tab[h, quarter].reshape(DEPTH, HS) for h in range(2)]
+        queries = pat[quarter, y].astype(F32)
         shares = []
         for h in range(2):
-            dots = jnp.sum(tables[h].astype(F32) * query_f[:, h * HS : (h + 1) * HS], axis=1, keepdims=True)
+            query_f = queries[ROWS - 2 + h : ROWS - 1 + h, :]
+            dots = jnp.sum(tables[h].astype(F32) * query_f, axis=1, keepdims=True)
             shares.append((dots * (1.0 / math.sqrt(HS))) * points_f)
         share = jnp.concatenate(shares, axis=1)
-        which, real = block_of(lax.broadcasted_iota(jnp.int32, (N_VARS, DEPTH), 1))
-        collect = jnp.where(
-            (which == lax.broadcasted_iota(jnp.int32, (N_VARS, DEPTH), 0)) & real, 1.0, 0.0
-        ).astype(BF16)
         scores = jnp.zeros((N_VARS, COLS), F32)
         for _ in range(3):
             piece = share.astype(BF16)
             share = share - piece.astype(F32)
-            scores = scores + jnp.dot(collect, piece, preferred_element_type=F32)
+            scores = scores + jnp.dot(collect[...], piece, preferred_element_type=F32)
         diagonal = lax.broadcasted_iota(jnp.int32, (N_VARS, N_VARS), 0) == lax.broadcasted_iota(
             jnp.int32, (N_VARS, N_VARS), 1
         )
@@ -291,11 +301,7 @@
         scores = jnp.where(keep > 0.0, scores, -1e30)
         expo = jnp.exp(scores - jnp.max(scores, axis=0, keepdims=True))
         weights = (expo / jnp.sum(expo, axis=0, keepdims=True)).astype(BF16)
-        which, real = block_of(lax.broadcasted_iota(jnp.int32, (DEPTH, N_VARS), 0))
-        expand = jnp.where(
-            (which == lax.broadcasted_iota(jnp.int32, (DEPTH, N_VARS), 1)) & real, 1.0, 0.0
-        ).astype(BF16)
-        mixed = jnp.dot(expand, weights, preferred_element_type=F32) * twice
+        mixed = jnp.dot(expand[...], weights, preferred_element_type=F32) * twice
         high = mixed.astype(BF16)
         low = (mixed - high.astype(F32)).astype(BF16)
         over_rows = (((0,), (0,)), ((), ()))
@@ -306,16 +312,8 @@
                 lax.dot_general(high[:, cols], tables[h], over_rows, preferred_element_type=F32)
                 + lax.dot_general(low[:, cols], tables[h], over_rows, preferred_element_type=F32)
             )
-        agg[var] = jnp.concatenate(merged, axis=1).astype(BF16)
-
-        for i in (1, 2, 3):
-            send(agg.at[var], agg.at[var], "agg", ("az", i), at_var(mod4(zl + i), y))
-        for i in (1, 3, 2):
-            send(agg.at[var], agg.at[var], "agg", "ay", at_var(zl, mod4(y + i)))
-
-    def features_y(j):
-        place = agg.at[mod4(zl - j) * 4 + y]
-        recv(place, ("az", j))
+        place = agg.at[quarter * 4 + y]
+        place[...] = jnp.concatenate(merged, axis=1).astype(BF16)
         for i in (1, 3, 2):
             send(place, place, "agg", "ay", at_var(zl, mod4(y + i)))
 
@@ -350,6 +348,10 @@
     def activate():
         hidden_ref[...] = jax.nn.gelu(part[...], approximate=True).astype(BF16)
 
+    def halves(a):
+        n = 2 if a == 2 else 1
+        return [slice(i * TOK // n, (i + 1) * TOK // n) for i in range(n)]
+
     def down_part(a, b):
         if a == 0 and b == 0:
             locals_[7].wait()
@@ -370,26 +372,28 @@
 
         @pl.when(away != 0)
         def _():
-            send(term.at[a % 4, b % 4], got_y.at[a % 4, away], "ry", ("ry", a % 4), at_var(zl, y_))
-
-    def down_sum(a):
-        a = a % 4
+            for half in halves(a):
+                src, dst = term.at[a % 4, b % 4, half], got_y.at[a % 4, away, half]
+                send(src, dst, "ry", ("ry", a % 4, half.start), at_var(zl, y_))
+
+    def down_sum(a, number=0):
+        a, half = a % 4, halves(a)[number]
         q = mod4(zh + a)
-        recv(got_y.at[a, 1:4], ("ry", a))
-        value = own_sum[a]
+        recv(got_y.at[a, 1:4, half], ("ry", a, half.start))
+        value = own_sum[a, half]
         for i in (1, 2, 3):
-            value = value + got_y[a, i].astype(F32)
+            value = value + got_y[a, i, half].astype(F32)
         away = mod4(zl - q)
 
         @pl.when(away == 0)
         def _():
-            total[...] = value
-
-        summed[a] = value.astype(BF16)
+            total[half] = value
+
+        summed[a, half] = value.astype(BF16)
 
         @pl.when(away != 0)
         def _():
-            send(summed.at[a], got_z.at[away], "rz", "rz", at_var(q, y))
+            send(summed.at[a, half], got_z.at[away, half], "rz", "rz", at_var(q, y))
 
     def all_sent():
         for m in (0, 1):
@@ -400,8 +404,9 @@
         sent(pat.at[0:3], "py")
         sent(tab_mid.at[0:3], "tz")
         sent(tab_mid.at[0:3], "ty")
+        sent(tab.at[0, 0:3], "tx")
         sent(tab.at[0], "ts")
-        sent(agg.at[0:15], "agg")
+        sent(agg.at[0:12], "agg")
 
     def finish():
         result = agg[var].astype(F32) + total[...]
@@ -424,10 +429,10 @@
         "XR": x_rest,
         "S": swap,
         "py": points_y,
-        "ty": table_y,
-        "ts": table_swap,
+        "tz": table_z,
+        "tx": table_x,
+        "tsib": table_swap,
         "agg": aggregate,
-        "ayz": features_y,
         "ln": layer_norm,
         "up": up_part,
         "hid": activate,
@@ -459,7 +464,9 @@
             vmem((ROWS, TOK), F32),
             vmem((4, 4, ROWS, HS), BF16),
             vmem((4, 4, ROWS, HS), BF16),
-            vmem((2, 4, 4, ROWS, HS), BF16),
+            vmem((2, 4, 4, 4, ROWS, HS), BF16),
+            vmem((N_VARS, DEPTH), BF16),
+            vmem((DEPTH, N_VARS), BF16),
             vmem((4, 4, ROWS, TOK), BF16),
             vmem((16, TOK, COLS), BF16),
             vmem((4, TOK, 1024), BF16),

time: 81.6 us -> 79.1 us (0.969)
  the two profiles are of different devices: /device:TPU:80 before, /device:TPU:37 now
where the time goes in v4:
time: 79.1 us; the launch traced here: 78.9 us
  Pallas kernels  77.5 us (98%)
  local copies, waits for them, and re-layouts  1.47 us (2%)
    pallas_call x1, Pallas kernels, shards(): pl.pallas_call(kernel, out_shape=jax.ShapeDtypeStruct((TOK, COLS), BF16),...  77.5 us

profile of v4, /device:TPU:37, one launch (start us, length us, event | category | flops | bytes accessed | tf_op | source)
XLA Modules:
  0.0 78.9 jit_solution(6433078346766907592)
XLA Ops:
  0.0 77.5 %shard_map.82 = bf16[128,256]{1,0:T(8,128)(2,1)} custom-call(bf16[6,4,128]{2,1,0:T(4,128)(2,1)} %pix_in.1, bf16[6,4,4096]{2,1,0:T(4,128)(2,1)} %emb_in.1, bf16[6,4096]{1,0:T(8,128)(2,1)} %bias_in.1, s32[96]{0:T(128)} %mask_in.1, bf16[256]{0:T(256)(128)(2,1)} %query_in.1, bf16[4096]{0:T(1024)(128)(2,1)} %gain_in.1, bf16[128,512]{1,0:T(8,128)(2,1)} %up_in.1, ...), custom_call_target="tpu_custom_call" | custom-call | tf_op jit(solution)/shard_map/pallas_call | solution.py:451
  77.5 1.5 %copy.10 = bf16[128,256]{1,0:T(8,128)(2,1)} copy(bf16[128,256]{1,0:T(8,128)(2,1)} %shard_map.82) | data formatting | bytes 131072

commit v5 on v4

--- a/solution.py
+++ b/solution.py
@@ -16,26 +16,28 @@
 DEPTH = 16 * ROWS
 TOK, COLS, D, FF = 128, 256, 4096, 512
 N_SENT, N_RECV = 15, 120
-SPLIT = (2, 4)
+SPLIT = (4, 4)
 SPLIT_NEAR = (2, 2)
 ORDER = (
-    ("pack",), ("start",), ("z0", 0), ("z0", 1), ("x0", 0), ("x0", 1), ("X", 0, 0, -1, 0), ("X", 0, 0, 1, 1),
-    ("XR", 0, 0, -1), ("XR", 0, 0, 1), ("py",), ("X", 1, 0, -1, 0), ("X", 1, 0, 1, 1), ("tz",), ("XR", 1, 0, -1),
-    ("XR", 1, 0, 1), ("XR", 0, 0, 2), ("XR", 1, 0, 2), ("Z", 0, -1, 0), ("Z", 0, 1, 1), ("z1", 0), ("z1", 1),
-    ("z1", 2), ("z1", 3), ("tx",), ("X", 0, -1, -1, 0), ("agg", 0), ("Z", 0, -1, 1), ("S", 0, -1, 0), ("Z", 0, 1, 0),
-    ("S", 0, 1, 0), ("X", 0, 1, 1, 1), ("tsib", -1), ("tsib", 1), ("Z2", 0, 0), ("S", 0, 2, 0), ("agg", -1),
-    ("agg", 1), ("Z", 1, -1, 0), ("X", 0, -1, 1, 1), ("XR", 0, -1, 1), ("Z", 1, 1, 3), ("tsib", 2), ("XR", 0, -1, -1),
-    ("XR", 0, 1, 1), ("agg", 2), ("X", 0, 1, -1, 0), ("XR", 0, 1, -1), ("Z", 1, -1, 1), ("Z", 1, 1, 2),
-    ("X", 0, 2, -1, 0), ("X", 0, 2, 1, 1), ("Z", 1, -1, 2), ("Z", 1, 1, 1), ("XR", 0, 2, -1), ("XR", 0, 2, 1),
-    ("X", 1, -1, -1, 0), ("XR", 0, -1, 2), ("Z", 1, -1, 3), ("S", 1, -1, 0), ("Z", 1, 1, 0), ("XR", 0, 1, 2),
-    ("S", 1, 1, 0), ("X", 1, 1, 1, 3), ("X", 1, -1, -1, 1), ("ln",), ("Z2", 1, 0), ("XR", 0, 2, 2), ("X", 1, 1, 1, 2),
-    ("up", 0), ("X", 1, -1, 1, 2), ("up", -1), ("X", 1, 1, -1, 1), ("up", 1), ("X", 1, -1, 1, 3), ("XR", 1, -1, 1),
-    ("Z2", 1, 1), ("S", 1, 2, 0), ("XR", 1, -1, -1), ("XR", 1, 1, 1), ("up", 2), ("X", 1, 1, -1, 0), ("XR", 1, 1, -1),
-    ("hid",), ("dp", 0, 0), ("X", 1, 2, 1, 3), ("dp", 0, -1), ("dp", 0, 1), ("X", 1, 2, -1, 0), ("dp", 0, 2),
-    ("dp", -1, 0), ("dp", -1, -1), ("dp", -1, 1), ("dp", 1, 0), ("dp", 1, -1), ("dp", 1, 1), ("dp", 2, 0),
-    ("X", 1, 2, -1, 1), ("XR", 1, -1, 2), ("XR", 1, 2, -1), ("X", 1, 2, 1, 2), ("dp", -1, 2), ("XR", 1, 1, 2),
-    ("XR", 1, 2, 1), ("dp", 2, -1), ("dp", 1, 2), ("dp", 2, 1), ("XR", 1, 2, 2), ("ds", 0), ("dp", 2, 2), ("ds", -1),
-    ("ds", 1), ("ds", 2, 0), ("sent",), ("ds", 2, 1), ("fin",),
+    ("x0", 0), ("z0", 0), ("pack",), ("z0", 1), ("start",), ("x0", 1), ("tz",), ("z0", 2), ("X", 0, 0, 1, 1),
+    ("X", 1, 0, -1, 0), ("Z", 0, 1, 3), ("py",), ("z0", 3), ("Z", 0, -1, 0), ("X", 1, 0, 1, 1), ("tx",),
+    ("X", 0, 0, -1, 0), ("X", 0, 1, 1, 3), ("XR", 0, 0, 1), ("Z", 0, -1, 1), ("Z", 0, 1, 2), ("agg", 0), ("z1", 0),
+    ("Z", 0, 1, 1), ("tsib", 1), ("tsib", -1), ("Z", 0, -1, 3), ("X", 0, -1, -1, 0), ("agg", -1), ("Z", 0, -1, 2),
+    ("XR", 0, 0, -1), ("X", 0, -1, -1, 1), ("z1", 1), ("Z", 0, 1, 0), ("z1", 2), ("X", 0, 1, -1, 1), ("agg", 1),
+    ("X", 0, 1, 1, 2), ("tsib", 2), ("XR", 1, 0, 1), ("Z2", 0, 1), ("z1", 3), ("Z2", 0, 0), ("agg", 2),
+    ("XR", 0, 0, 2), ("X", 0, -1, 1, 3), ("Z", 1, 1, 3), ("X", 0, 1, -1, 0), ("S", -1, 0), ("X", 0, -1, 1, 2),
+    ("X", 0, 2, -1, 0), ("X", 0, 2, 1, 3), ("X", 0, 2, -1, 1), ("S", 1, 0), ("X", 0, 2, 1, 2), ("Z", 1, 1, 1),
+    ("XR", 0, 1, -1), ("Z", 1, -1, 0), ("ln",), ("Z", 1, -1, 1), ("XR", 1, 0, 2), ("XR", 0, 2, 1), ("S", 2, 0),
+    ("XR", 0, 1, 2), ("XR", 0, -1, -1), ("XR", 0, -1, 1), ("Z", 1, 1, 2), ("XR", 0, 2, 2), ("Z", 1, -1, 2),
+    ("XR", 0, 1, 1), ("XR", 0, 2, -1), ("Z", 1, -1, 3), ("up", 0), ("XR", 1, 0, -1), ("Z", 1, 1, 0), ("XR", 0, -1, 2),
+    ("X", 1, -1, -1, 0), ("up", 1), ("up", 2), ("up", -1), ("hid",), ("X", 1, -1, -1, 1), ("X", 1, 1, 1, 3),
+    ("Z2", 1, 0), ("dp", 0, 0), ("X", 1, 1, -1, 1), ("X", 1, -1, 1, 2), ("dp", -1, 0), ("X", 1, -1, 1, 3),
+    ("dp", 0, 2), ("dp", 0, 1), ("dp", 1, 0), ("Z2", 1, 1), ("X", 1, 1, -1, 0), ("X", 1, 1, 1, 2), ("dp", 2, 0),
+    ("XR", 1, -1, -1), ("XR", 1, -1, 1), ("X", 1, 2, 1, 3), ("dp", 0, -1), ("X", 1, 2, -1, 0), ("XR", 1, 1, -1),
+    ("XR", 1, 1, 1), ("dp", -1, 1), ("dp", -1, -1), ("XR", 1, -1, 2), ("dp", -1, 2), ("dp", 1, 1), ("X", 1, 2, -1, 1),
+    ("X", 1, 2, 1, 2), ("dp", 1, -1), ("XR", 1, 2, -1), ("XR", 1, 1, 2), ("dp", 1, 2), ("dp", 2, -1), ("XR", 1, 2, 1),
+    ("XR", 1, 2, 2), ("ds", 0), ("dp", 2, 2), ("dp", 2, 1), ("ds", -1), ("ds", 1), ("ds", 2, 0), ("sent",),
+    ("ds", 2, 1), ("fin",),
 )
 
 
@@ -48,7 +50,7 @@
 def kernel(
     pix_in, emb_in, bias_in, mask_in, query_in, gain_in, up_in, down_in, out,
     pix, emb, bias, mask, query, gain, rows_f, pix_f,
-    tab_out, tab_mid, tab, collect, expand, pat, agg, norm, up, down, own_sum, term, got_y, got_z, summed, hidden_ref, part, total,
+    tab_out, tab_mid, tab, collect, expand, pat, agg, norm, up, down, own_sum, term, got_y, got_z, summed, hidden, part, total,
     local_sem, send_sem, recv_sem,
 ):
     var, seq = lax.axis_index("var"), lax.axis_index("seq")
@@ -82,7 +84,7 @@
             (query_in, query),
             (gain_in, gain),
             (up_in, up.at[zh, x, core]),
-            (down_in, down.at[zh, x, :, pl.ds(pl.multiple_of(core * HS, HS), HS)]),
+            (down_in, down.at[zh, x]),
         )
     ):
         locals_.append(pltpu.make_async_copy(src, dst, local_sem.at[i]))
@@ -93,7 +95,7 @@
     peers += [at_var(mod4(zl + i), y) for i in (1, 2, 3)]
     peers += [at_var(zl, mod4(y + i)) for i in (1, 2, 3)]
     peers += [at_seq(1, 0, core), at_seq(-1, 0, core)]
-    peers += [at_seq(0, i, core) for i in (1, 2, 3)]
+    peers += [at_seq(0, i, core) for i in (1, 3)]
     for peer in peers:
         pl.semaphore_signal(barrier, inc=1, device_id=peer, device_id_type=MESH)
 
@@ -134,13 +136,12 @@
     def block(m, a, b, core_):
         if m == 0:
             return up.at[mod4(zh + a), mod4(x + b), core_]
-        return down.at[mod4(zh + a), mod4(x + b), :, pl.ds(pl.multiple_of(core_ * HS, HS), HS)]
+        return down.at[mod4(zh + a), mod4(x + b)]
 
     def piece(m, a, b, p, count=1):
         if m == 0:
             return block(m, a, b, core).at[rows_of(m, a, p, count)]
-        cols = pl.ds(pl.multiple_of(core * HS, HS), HS)
-        return down.at[mod4(zh + a), mod4(x + b), rows_of(m, a, p, count), cols]
+        return down.at[mod4(zh + a), mod4(x + b), rows_of(m, a, p, count)]
 
     def z_key(m, a, p):
         return ("z", m, a % 4, p)
@@ -158,7 +159,7 @@
             if m == 0:
                 dst = up.at[zh, x, core].at[rows]
             else:
-                dst = down.at[zh, x, rows, pl.ds(pl.multiple_of(core * HS, HS), HS)]
+                dst = down.at[zh, x, rows]
         else:
             src = dst = piece(m, a, 0, p)
         send(src, dst, ("z", m), z_key(m, a - step, p), at_seq(step, 0, core))
@@ -170,13 +171,9 @@
             src = (up_in, down_in)[m].at[rows_of(m, 0, p)]
         send(src, dst, ("x", m), x_key(m, a, b - step, p), at_seq(0, step, core))
 
-    def s_key(m, a, b):
-        return ("s", m, a % 4, b % 4 if m == 1 and a else 0)
-
-    def swap(m, a, b):
-        place = block(m, a, b, core)
-        src = (up_in, down_in)[m] if a == 0 and b == 0 else place
-        send(src, place, ("s", m), s_key(m, a, b), sibling)
+    def swap(a, b):
+        place = block(0, a, b, core)
+        send(up_in if a == 0 and b == 0 else place, place, "s", ("s", a % 4), sibling)
 
     def z_first(m, i):
         z_send(m, 0, i, "z+")
@@ -187,7 +184,8 @@
         for i in range(n):
             x_send(m, 0, 0, i, "x+")
             x_send(m, 0, 0, n - 1 - i, "x-")
-        swap(m, 0, 0)
+        if m == 0:
+            swap(0, 0)
 
     def z_piece(m, a, p):
         n = pieces(m, a)
@@ -216,7 +214,8 @@
         n = pieces(m, a)
         first, count = {-1: (n // 2, n // 2), 1: (0, n // 2), 2: (0, n)}[b]
         recv(piece(m, a, b, first, count), x_key(m, a, b, first))
-        swap(m, a, b)
+        if m == 0:
+            swap(a, b)
 
     def pack():
         for i in (0, 1, 2, 4):
@@ -258,13 +257,16 @@
 
     def table_x():
         recv(tab.at[core, x, 0:3], "tz")
-        for b in (1, -1, 2):
+        for b in (1, -1):
             send(tab.at[core, x], tab.at[core, x], "tx", ("tx", -b % 4), at_seq(0, b, core))
         send(tab.at[core, x], tab.at[core, x], "ts", ("ts", 0), sibling)
 
     def table_swap(b):
         place = tab.at[core, mod4(x + b)]
         recv(place, ("tx", b % 4))
+        if b != 2:
+            part = place.at[pl.ds(0 if b == -1 else 2, 2)]
+            send(part, part, "tx", ("tx", 2), at_seq(0, -b, core))
         send(place, place, "ts", ("ts", b % 4), sibling)
 
     def aggregate(b):
@@ -341,12 +343,13 @@
         if a == 0:
             locals_[6].wait()
         q = mod4(zh + a)
-        recv(up.at[q, :, other], s_key(0, a, 0))
+        recv(up.at[q, :, other], ("s", a % 4))
         value = jnp.dot(norm[q], up[q].reshape(1024, FF), preferred_element_type=F32)
         part[...] = value if a == 0 else part[...] + value
 
     def activate():
-        hidden_ref[...] = jax.nn.gelu(part[...], approximate=True).astype(BF16)
+        hidden[core] = jax.nn.gelu(part[...], approximate=True).astype(BF16)
+        send(hidden.at[core], hidden.at[core], "h", "h", sibling)
 
     def halves(a):
         n = 2 if a == 2 else 1
@@ -355,41 +358,43 @@
     def down_part(a, b):
         if a == 0 and b == 0:
             locals_[7].wait()
+            recv(hidden.at[other], "h")
         q, y_ = mod4(zh + a), mod4(x + b)
-        cols = pl.ds(pl.multiple_of(other * HS, HS), HS)
-        if a:
-            recv(down.at[q, y_, :, cols], s_key(1, a, b))
-        elif b == 0:
-            recv(down.at[q, :, :, cols], s_key(1, a, b))
-        value = jnp.dot(hidden_ref[...], down[q, y_], preferred_element_type=F32)
         away = mod4(y_ - y)
+        value = jnp.dot(hidden[...].reshape(2 * TOK, FF), down[q, y_], preferred_element_type=F32)
+        term[a % 4, b % 4] = value.astype(BF16).reshape(2, TOK, HS)
+
+        def deliver(core_):
+            for half in halves(a):
+                src, dst = term.at[a % 4, b % 4, core_, half], got_y.at[a % 4, away * 2 + core, half]
+                send(src, dst, "ry", ("ry", a % 4, half.start), (zl * 4 + y_, zh * 8 + x * 2 + core_))
+
+        deliver(other)
 
         @pl.when(away == 0)
         def _():
-            own_sum[a % 4] = value
-
-        term[a % 4, b % 4] = value.astype(BF16)
+            own_sum[a % 4] = term[a % 4, b % 4, core].astype(F32)
 
         @pl.when(away != 0)
         def _():
-            for half in halves(a):
-                src, dst = term.at[a % 4, b % 4, half], got_y.at[a % 4, away, half]
-                send(src, dst, "ry", ("ry", a % 4, half.start), at_var(zl, y_))
+            deliver(core)
 
     def down_sum(a, number=0):
         a, half = a % 4, halves(a)[number]
         q = mod4(zh + a)
-        recv(got_y.at[a, 1:4, half], ("ry", a, half.start))
-        value = own_sum[a, half]
-        for i in (1, 2, 3):
-            value = value + got_y[a, i, half].astype(F32)
         away = mod4(zl - q)
-
-        @pl.when(away == 0)
-        def _():
-            total[half] = value
-
-        summed[a, half] = value.astype(BF16)
+        recv(got_y.at[a, 0:7, half], ("ry", a, half.start))
+        for core_ in (core, other):
+            cols = pl.ds(pl.multiple_of(core_ * HS, HS), HS)
+            value = own_sum[a, half] if core_ is core else got_y[a, other, half].astype(F32)
+            for i in (1, 2, 3):
+                value = value + got_y[a, i * 2 + core_, half].astype(F32)
+
+            @pl.when(away == 0)
+            def _():
+                total[half, cols] = value
+
+            summed[a, half, cols] = value.astype(BF16)
 
         @pl.when(away != 0)
         def _():
@@ -399,7 +404,8 @@
         for m in (0, 1):
             sent(up.at[0, 0:3, 0], ("z", m))
             sent(up.at[0:3, :, 0], ("x", m))
-            sent(up.at[0:2], ("s", m))
+        sent(up.at[0:2], "s")
+        sent(hidden.at[0], "h")
         sent(pat.at[0, 0:3], "pz")
         sent(pat.at[0:3], "py")
         sent(tab_mid.at[0:3], "tz")
@@ -414,7 +420,7 @@
         for i in (1, 2, 3):
             result = result + got_z[i].astype(F32)
         out[...] = result.astype(BF16)
-        sent(got_y.at[0:3], "ry")
+        sent(got_y.at[:, 0:7], "ry")
         sent(got_z.at[0:3], "rz")
 
     steps = {
@@ -471,13 +477,13 @@
             vmem((16, TOK, COLS), BF16),
             vmem((4, TOK, 1024), BF16),
             vmem((4, 4, 2, 128, FF), BF16),
-            vmem((4, 4, FF, COLS), BF16),
-            vmem((4, TOK, COLS), F32),
-            vmem((4, 4, TOK, COLS), BF16),
-            vmem((4, 4, TOK, COLS), BF16),
+            vmem((4, 4, FF, HS), BF16),
+            vmem((4, TOK, HS), F32),
+            vmem((4, 4, 2, TOK, HS), BF16),
+            vmem((4, 8, TOK, HS), BF16),
             vmem((4, TOK, COLS), BF16),
             vmem((4, TOK, COLS), BF16),
-            vmem((TOK, FF), BF16),
+            vmem((2, TOK, FF), BF16),
             vmem((TOK, FF), F32),
             vmem((TOK, COLS), F32),
             pltpu.SemaphoreType.DMA((8,)),

time: 79.1 us -> 76.9 us (0.972)
  the two profiles are of different devices: /device:TPU:37 before, /device:TPU:72 now
where the time goes in v5:
time: 76.9 us; the launch traced here: 76.8 us
  Pallas kernels  75.3 us (98%)
  local copies, waits for them, and re-layouts  1.47 us (2%)
    pallas_call x1, Pallas kernels, shards(): pl.pallas_call(kernel, out_shape=jax.ShapeDtypeStruct((TOK, COLS), BF16),...  75.3 us

profile of v5, /device:TPU:72, one launch (start us, length us, event | category | flops | bytes accessed | tf_op | source)
XLA Modules:
  0.0 76.8 jit_solution(17549607556495230866)
XLA Ops:
  0.0 75.3 %shard_map.82 = bf16[128,256]{1,0:T(8,128)(2,1)} custom-call(bf16[6,4,128]{2,1,0:T(4,128)(2,1)} %pix_in.1, bf16[6,4,4096]{2,1,0:T(4,128)(2,1)} %emb_in.1, bf16[6,4096]{1,0:T(8,128)(2,1)} %bias_in.1, s32[96]{0:T(128)} %mask_in.1, bf16[256]{0:T(256)(128)(2,1)} %query_in.1, bf16[4096]{0:T(1024)(128)(2,1)} %gain_in.1, bf16[128,512]{1,0:T(8,128)(2,1)} %up_in.1, ...), custom_call_target="tpu_custom_call" | custom-call | tf_op jit(solution)/shard_map/pallas_call | solution.py:457
  75.3 1.5 %copy.10 = bf16[128,256]{1,0:T(8,128)(2,1)} copy(bf16[128,256]{1,0:T(8,128)(2,1)} %shard_map.82) | data formatting | bytes 131072

commit v6 on v5

--- a/solution.py
+++ b/solution.py
@@ -15,28 +15,28 @@
 ROWS = 32
 DEPTH = 16 * ROWS
 TOK, COLS, D, FF = 128, 256, 4096, 512
-N_SENT, N_RECV = 15, 120
+N_SENT, N_RECV = 15, 99
 SPLIT = (4, 4)
 SPLIT_NEAR = (2, 2)
 ORDER = (
-    ("x0", 0), ("z0", 0), ("pack",), ("z0", 1), ("start",), ("x0", 1), ("tz",), ("z0", 2), ("X", 0, 0, 1, 1),
-    ("X", 1, 0, -1, 0), ("Z", 0, 1, 3), ("py",), ("z0", 3), ("Z", 0, -1, 0), ("X", 1, 0, 1, 1), ("tx",),
-    ("X", 0, 0, -1, 0), ("X", 0, 1, 1, 3), ("XR", 0, 0, 1), ("Z", 0, -1, 1), ("Z", 0, 1, 2), ("agg", 0), ("z1", 0),
-    ("Z", 0, 1, 1), ("tsib", 1), ("tsib", -1), ("Z", 0, -1, 3), ("X", 0, -1, -1, 0), ("agg", -1), ("Z", 0, -1, 2),
-    ("XR", 0, 0, -1), ("X", 0, -1, -1, 1), ("z1", 1), ("Z", 0, 1, 0), ("z1", 2), ("X", 0, 1, -1, 1), ("agg", 1),
-    ("X", 0, 1, 1, 2), ("tsib", 2), ("XR", 1, 0, 1), ("Z2", 0, 1), ("z1", 3), ("Z2", 0, 0), ("agg", 2),
-    ("XR", 0, 0, 2), ("X", 0, -1, 1, 3), ("Z", 1, 1, 3), ("X", 0, 1, -1, 0), ("S", -1, 0), ("X", 0, -1, 1, 2),
-    ("X", 0, 2, -1, 0), ("X", 0, 2, 1, 3), ("X", 0, 2, -1, 1), ("S", 1, 0), ("X", 0, 2, 1, 2), ("Z", 1, 1, 1),
-    ("XR", 0, 1, -1), ("Z", 1, -1, 0), ("ln",), ("Z", 1, -1, 1), ("XR", 1, 0, 2), ("XR", 0, 2, 1), ("S", 2, 0),
-    ("XR", 0, 1, 2), ("XR", 0, -1, -1), ("XR", 0, -1, 1), ("Z", 1, 1, 2), ("XR", 0, 2, 2), ("Z", 1, -1, 2),
-    ("XR", 0, 1, 1), ("XR", 0, 2, -1), ("Z", 1, -1, 3), ("up", 0), ("XR", 1, 0, -1), ("Z", 1, 1, 0), ("XR", 0, -1, 2),
-    ("X", 1, -1, -1, 0), ("up", 1), ("up", 2), ("up", -1), ("hid",), ("X", 1, -1, -1, 1), ("X", 1, 1, 1, 3),
-    ("Z2", 1, 0), ("dp", 0, 0), ("X", 1, 1, -1, 1), ("X", 1, -1, 1, 2), ("dp", -1, 0), ("X", 1, -1, 1, 3),
-    ("dp", 0, 2), ("dp", 0, 1), ("dp", 1, 0), ("Z2", 1, 1), ("X", 1, 1, -1, 0), ("X", 1, 1, 1, 2), ("dp", 2, 0),
-    ("XR", 1, -1, -1), ("XR", 1, -1, 1), ("X", 1, 2, 1, 3), ("dp", 0, -1), ("X", 1, 2, -1, 0), ("XR", 1, 1, -1),
-    ("XR", 1, 1, 1), ("dp", -1, 1), ("dp", -1, -1), ("XR", 1, -1, 2), ("dp", -1, 2), ("dp", 1, 1), ("X", 1, 2, -1, 1),
-    ("X", 1, 2, 1, 2), ("dp", 1, -1), ("XR", 1, 2, -1), ("XR", 1, 1, 2), ("dp", 1, 2), ("dp", 2, -1), ("XR", 1, 2, 1),
-    ("XR", 1, 2, 2), ("ds", 0), ("dp", 2, 2), ("dp", 2, 1), ("ds", -1), ("ds", 1), ("ds", 2, 0), ("sent",),
+    ("pack",), ("start",), ("z0", 0), ("z0", 1), ("tz",), ("z0", 2), ("x0", 0), ("z0", 3), ("py",), ("x0", 1),
+    ("Z", 0, -1, 1), ("Z", 0, 1, 3), ("X", 0, 0, -1, 0), ("XR", 0, 0, -1), ("Z", 0, 1, 2), ("tx",), ("Z", 0, -1, 0),
+    ("X", 0, 0, 1, 1), ("agg", 0), ("Z", 0, 1, 1), ("X", 0, 1, 1, 3), ("XR", 0, 0, 1), ("X", 1, 0, -1, 0), ("z1", 0),
+    ("tsib", 1), ("z1", 1), ("Z", 0, 1, 0), ("tsib", -1), ("Z", 0, -1, 2), ("agg", -1), ("z1", 2), ("X", 0, 1, 1, 2),
+    ("X", 0, 1, -1, 1), ("Z", 0, -1, 3), ("Z2", 0, 0), ("agg", 1), ("z1", 3), ("X", 1, 0, 1, 1), ("Z2", 0, 1),
+    ("X", 0, -1, 1, 2), ("tsib", 2), ("S", -1, 0), ("XR", 0, 0, 2), ("X", 0, -1, -1, 0), ("agg", 2),
+    ("X", 0, 2, -1, 0), ("X", 0, 2, -1, 1), ("XR", 0, 1, 1), ("Z", 1, -1, 0), ("X", 0, -1, -1, 1), ("S", 2, 0),
+    ("XR", 0, -1, -1), ("X", 0, 2, 1, 3), ("X", 0, -1, 1, 3), ("X", 0, 2, 1, 2), ("X", 0, 1, -1, 0), ("S", 1, 0),
+    ("XR", 0, 1, -1), ("Z", 1, 1, 3), ("Z", 1, -1, 2), ("Z", 1, -1, 1), ("Z", 1, 1, 1), ("ln",), ("XR", 0, 1, 2),
+    ("XR", 0, -1, 1), ("Z", 1, 1, 2), ("XR", 1, 0, 2), ("X", 1, -1, -1, 0), ("XR", 0, 2, 2), ("XR", 0, -1, 2),
+    ("XR", 1, 0, -1), ("up", 0), ("XR", 0, 2, 1), ("up", 1), ("Z", 1, -1, 3), ("XR", 0, 2, -1), ("X", 1, -1, -1, 1),
+    ("up", -1), ("X", 1, -1, 1, 2), ("up", 2), ("X", 1, 1, 1, 3), ("hid",), ("Z", 1, 1, 0), ("dp", 0, 0),
+    ("dp", 1, 0), ("X", 1, -1, 1, 3), ("XR", 1, 0, 1), ("X", 1, 1, 1, 2), ("dp", -1, 0), ("X", 1, 1, -1, 1),
+    ("Z2", 1, 0), ("XR", 1, -1, -1), ("X", 1, 1, -1, 0), ("dp", 0, 1), ("Z2", 1, 1), ("dp", -1, -1), ("XR", 1, 1, -1),
+    ("dp", 0, 2), ("XR", 1, -1, 2), ("XR", 1, 1, 1), ("dp", 0, -1), ("dp", -1, 2), ("X", 1, 2, 1, 3),
+    ("XR", 1, -1, 1), ("dp", 1, -1), ("dp", -1, 1), ("X", 1, 2, -1, 0), ("X", 1, 2, -1, 1), ("XR", 1, 1, 2),
+    ("X", 1, 2, 1, 2), ("dp", 1, 1), ("dp", 1, 2), ("XR", 1, 2, 1), ("dp", 2, 1), ("dp", 2, 0), ("XR", 1, 2, -1),
+    ("ds", 0), ("dp", 2, -1), ("XR", 1, 2, 2), ("dp", 2, 2), ("ds", -1), ("ds", 1), ("ds", 2, 0), ("sent",),
     ("ds", 2, 1), ("fin",),
 )
 
@@ -73,6 +73,15 @@
         return (lax.rem(z_, 4) * 4 + y, (z_ // 4) * 8 + x * 2 + core)
 
     sibling = at_seq(0, 0, other)
+
+    barrier = pltpu.get_barrier_semaphore()
+    peers = [at_z(1), at_z(-1), at_z(2), at_z(-2), sibling]
+    peers += [at_var(mod4(zl + i), y) for i in (1, 2, 3)]
+    peers += [at_var(zl, mod4(y + i)) for i in (1, 2, 3)]
+    peers += [at_seq(1, 0, core), at_seq(-1, 0, core)]
+    peers += [at_seq(0, i, core) for i in (1, 3)]
+    for peer in peers:
+        pl.semaphore_signal(barrier, inc=1, device_id=peer, device_id_type=MESH)
 
     locals_ = []
     for i, (src, dst) in enumerate(
@@ -89,15 +98,6 @@
     ):
         locals_.append(pltpu.make_async_copy(src, dst, local_sem.at[i]))
         locals_[-1].start()
-
-    barrier = pltpu.get_barrier_semaphore()
-    peers = [at_z(1), at_z(-1), at_z(2), at_z(-2), sibling]
-    peers += [at_var(mod4(zl + i), y) for i in (1, 2, 3)]
-    peers += [at_var(zl, mod4(y + i)) for i in (1, 2, 3)]
-    peers += [at_seq(1, 0, core), at_seq(-1, 0, core)]
-    peers += [at_seq(0, i, core) for i in (1, 3)]
-    for peer in peers:
-        pl.semaphore_signal(barrier, inc=1, device_id=peer, device_id_type=MESH)
 
     groups, keys = {}, {}
 

time: 76.9 us -> 76.5 us (level)
  the two profiles are of different devices: /device:TPU:72 before, /device:TPU:80 now
where the time goes in v6:
time: 76.5 us; the launch traced here: 76.4 us
  Pallas kernels  74.9 us (98%)
  local copies, waits for them, and re-layouts  1.47 us (2%)
    pallas_call x1, Pallas kernels, shards(): pl.pallas_call(kernel, out_shape=jax.ShapeDtypeStruct((TOK, COLS), BF16),...  74.9 us

profile of v6, /device:TPU:80, one launch (start us, length us, event | category | flops | bytes accessed | tf_op | source)
XLA Modules:
  0.0 76.4 jit_solution(7567941492524424880)
XLA Ops:
  0.0 74.9 %shard_map.82 = bf16[128,256]{1,0:T(8,128)(2,1)} custom-call(bf16[6,4,128]{2,1,0:T(4,128)(2,1)} %pix_in.1, bf16[6,4,4096]{2,1,0:T(4,128)(2,1)} %emb_in.1, bf16[6,4096]{1,0:T(8,128)(2,1)} %bias_in.1, s32[96]{0:T(128)} %mask_in.1, bf16[256]{0:T(256)(128)(2,1)} %query_in.1, bf16[4096]{0:T(1024)(128)(2,1)} %gain_in.1, bf16[128,512]{1,0:T(8,128)(2,1)} %up_in.1, ...), custom_call_target="tpu_custom_call" | custom-call | tf_op jit(solution)/shard_map/pallas_call | solution.py:457
  74.9 1.5 %copy.10 = bf16[128,256]{1,0:T(8,128)(2,1)} copy(bf16[128,256]{1,0:T(8,128)(2,1)} %shard_map.82) | data formatting | bytes 131072

commit v7 on v6

--- a/solution.py
+++ b/solution.py
@@ -19,24 +19,24 @@
 SPLIT = (4, 4)
 SPLIT_NEAR = (2, 2)
 ORDER = (
-    ("pack",), ("start",), ("z0", 0), ("z0", 1), ("tz",), ("z0", 2), ("x0", 0), ("z0", 3), ("py",), ("x0", 1),
-    ("Z", 0, -1, 1), ("Z", 0, 1, 3), ("X", 0, 0, -1, 0), ("XR", 0, 0, -1), ("Z", 0, 1, 2), ("tx",), ("Z", 0, -1, 0),
-    ("X", 0, 0, 1, 1), ("agg", 0), ("Z", 0, 1, 1), ("X", 0, 1, 1, 3), ("XR", 0, 0, 1), ("X", 1, 0, -1, 0), ("z1", 0),
-    ("tsib", 1), ("z1", 1), ("Z", 0, 1, 0), ("tsib", -1), ("Z", 0, -1, 2), ("agg", -1), ("z1", 2), ("X", 0, 1, 1, 2),
-    ("X", 0, 1, -1, 1), ("Z", 0, -1, 3), ("Z2", 0, 0), ("agg", 1), ("z1", 3), ("X", 1, 0, 1, 1), ("Z2", 0, 1),
-    ("X", 0, -1, 1, 2), ("tsib", 2), ("S", -1, 0), ("XR", 0, 0, 2), ("X", 0, -1, -1, 0), ("agg", 2),
-    ("X", 0, 2, -1, 0), ("X", 0, 2, -1, 1), ("XR", 0, 1, 1), ("Z", 1, -1, 0), ("X", 0, -1, -1, 1), ("S", 2, 0),
-    ("XR", 0, -1, -1), ("X", 0, 2, 1, 3), ("X", 0, -1, 1, 3), ("X", 0, 2, 1, 2), ("X", 0, 1, -1, 0), ("S", 1, 0),
-    ("XR", 0, 1, -1), ("Z", 1, 1, 3), ("Z", 1, -1, 2), ("Z", 1, -1, 1), ("Z", 1, 1, 1), ("ln",), ("XR", 0, 1, 2),
-    ("XR", 0, -1, 1), ("Z", 1, 1, 2), ("XR", 1, 0, 2), ("X", 1, -1, -1, 0), ("XR", 0, 2, 2), ("XR", 0, -1, 2),
-    ("XR", 1, 0, -1), ("up", 0), ("XR", 0, 2, 1), ("up", 1), ("Z", 1, -1, 3), ("XR", 0, 2, -1), ("X", 1, -1, -1, 1),
-    ("up", -1), ("X", 1, -1, 1, 2), ("up", 2), ("X", 1, 1, 1, 3), ("hid",), ("Z", 1, 1, 0), ("dp", 0, 0),
-    ("dp", 1, 0), ("X", 1, -1, 1, 3), ("XR", 1, 0, 1), ("X", 1, 1, 1, 2), ("dp", -1, 0), ("X", 1, 1, -1, 1),
-    ("Z2", 1, 0), ("XR", 1, -1, -1), ("X", 1, 1, -1, 0), ("dp", 0, 1), ("Z2", 1, 1), ("dp", -1, -1), ("XR", 1, 1, -1),
-    ("dp", 0, 2), ("XR", 1, -1, 2), ("XR", 1, 1, 1), ("dp", 0, -1), ("dp", -1, 2), ("X", 1, 2, 1, 3),
-    ("XR", 1, -1, 1), ("dp", 1, -1), ("dp", -1, 1), ("X", 1, 2, -1, 0), ("X", 1, 2, -1, 1), ("XR", 1, 1, 2),
-    ("X", 1, 2, 1, 2), ("dp", 1, 1), ("dp", 1, 2), ("XR", 1, 2, 1), ("dp", 2, 1), ("dp", 2, 0), ("XR", 1, 2, -1),
-    ("ds", 0), ("dp", 2, -1), ("XR", 1, 2, 2), ("dp", 2, 2), ("ds", -1), ("ds", 1), ("ds", 2, 0), ("sent",),
+    ("x0", 0), ("z0", 0), ("pack",), ("z0", 1), ("start",), ("x0", 1), ("tz",), ("z0", 2), ("X", 0, 0, 1, 1),
+    ("X", 1, 0, -1, 0), ("Z", 0, 1, 3), ("py",), ("z0", 3), ("Z", 0, -1, 0), ("X", 1, 0, 1, 1), ("tx",),
+    ("X", 0, 0, -1, 0), ("XR", 0, 0, 1), ("Z", 0, -1, 1), ("Z", 0, 1, 2), ("X", 0, 1, 1, 3), ("agg", 0),
+    ("XR", 1, 0, 1), ("z1", 0), ("Z", 0, 1, 1), ("tsib", 1), ("tsib", -1), ("Z", 0, -1, 3), ("X", 0, -1, -1, 0),
+    ("agg", -1), ("Z", 0, -1, 2), ("XR", 0, 0, -1), ("X", 0, -1, -1, 1), ("z1", 1), ("Z", 0, 1, 0), ("z1", 2),
+    ("X", 0, 1, -1, 1), ("agg", 1), ("tsib", 2), ("Z2", 0, 1), ("z1", 3), ("X", 0, 1, 1, 2), ("Z2", 0, 0), ("agg", 2),
+    ("XR", 0, 0, 2), ("X", 0, -1, 1, 3), ("Z", 1, 1, 3), ("X", 0, 1, -1, 0), ("S", -1, 0), ("X", 0, -1, 1, 2),
+    ("X", 0, 2, -1, 0), ("X", 0, 2, 1, 3), ("X", 0, 2, -1, 1), ("S", 1, 0), ("X", 0, 2, 1, 2), ("Z", 1, 1, 1),
+    ("XR", 0, 1, -1), ("XR", 1, 0, -1), ("Z", 1, -1, 0), ("ln",), ("Z", 1, -1, 1), ("XR", 1, 0, 2), ("XR", 0, 2, 1),
+    ("S", 2, 0), ("XR", 0, 1, 2), ("XR", 0, -1, -1), ("XR", 0, -1, 1), ("Z", 1, 1, 2), ("XR", 0, 2, 2),
+    ("Z", 1, -1, 2), ("XR", 0, 1, 1), ("XR", 0, 2, -1), ("Z", 1, -1, 3), ("up", 0), ("Z", 1, 1, 0), ("XR", 0, -1, 2),
+    ("up", 1), ("up", 2), ("up", -1), ("hid",), ("X", 1, -1, -1, 1), ("X", 1, 1, 1, 3), ("Z2", 1, 0), ("dp", 0, 0),
+    ("X", 1, -1, -1, 0), ("X", 1, 1, -1, 1), ("X", 1, -1, 1, 2), ("dp", -1, 0), ("X", 1, -1, 1, 3), ("dp", 0, 2),
+    ("dp", 0, 1), ("dp", 1, 0), ("Z2", 1, 1), ("X", 1, 1, -1, 0), ("X", 1, 1, 1, 2), ("dp", 2, 0), ("dp", 0, -1),
+    ("XR", 1, -1, -1), ("XR", 1, -1, 1), ("X", 1, 2, 1, 3), ("X", 1, 2, -1, 0), ("XR", 1, 1, -1), ("XR", 1, 1, 1),
+    ("dp", -1, 1), ("dp", -1, -1), ("XR", 1, -1, 2), ("dp", -1, 2), ("dp", 1, 1), ("X", 1, 2, -1, 1),
+    ("X", 1, 2, 1, 2), ("dp", 1, -1), ("XR", 1, 2, -1), ("XR", 1, 1, 2), ("dp", 1, 2), ("dp", 2, -1), ("XR", 1, 2, 1),
+    ("XR", 1, 2, 2), ("ds", 0), ("dp", 2, 2), ("dp", 2, 1), ("ds", -1), ("ds", 1), ("ds", 2, 0), ("sent",),
     ("ds", 2, 1), ("fin",),
 )
 
@@ -124,6 +124,8 @@
         copy_of(view, view, group, next(iter(keys)), sibling).wait_send()
 
     pl.semaphore_wait(barrier, len(peers))
+    for i in (6, 7):
+        locals_[i].wait()
 
 
     def pieces(m, a):
@@ -155,11 +157,10 @@
         step = {"z+": 1, "z-": -1}[way]
         if a == 0:
             rows = rows_of(m, 1, p)
-            src = (up_in, down_in)[m].at[rows]
             if m == 0:
-                dst = up.at[zh, x, core].at[rows]
+                src = dst = up.at[zh, x, core].at[rows]
             else:
-                dst = down.at[zh, x, rows]
+                src = dst = down.at[zh, x, rows]
         else:
             src = dst = piece(m, a, 0, p)
         send(src, dst, ("z", m), z_key(m, a - step, p), at_seq(step, 0, core))
@@ -167,13 +168,11 @@
     def x_send(m, a, b, p, way):
         step = {"x+": 1, "x-": -1}[way]
         src = dst = piece(m, a, b, p)
-        if a == 0 and b == 0:
-            src = (up_in, down_in)[m].at[rows_of(m, 0, p)]
         send(src, dst, ("x", m), x_key(m, a, b - step, p), at_seq(0, step, core))
 
     def swap(a, b):
         place = block(0, a, b, core)
-        send(up_in if a == 0 and b == 0 else place, place, "s", ("s", a % 4), sibling)
+        send(place, place, "s", ("s", a % 4), sibling)
 
     def z_first(m, i):
         z_send(m, 0, i, "z+")
@@ -340,8 +339,6 @@
             ).astype(BF16)
 
     def up_part(a):
-        if a == 0:
-            locals_[6].wait()
         q = mod4(zh + a)
         recv(up.at[q, :, other], ("s", a % 4))
         value = jnp.dot(norm[q], up[q].reshape(1024, FF), preferred_element_type=F32)
@@ -357,7 +354,6 @@
 
     def down_part(a, b):
         if a == 0 and b == 0:
-            locals_[7].wait()
             recv(hidden.at[other], "h")
         q, y_ = mod4(zh + a), mod4(x + b)
         away = mod4(y_ - y)

time: 76.5 us -> 75.7 us (0.990)
  the two profiles are of different devices: /device:TPU:80 before, /device:TPU:72 now
where the time goes in v7:
time: 75.7 us; the launch traced here: 75.5 us
  Pallas kernels  74 us (98%)
  local copies, waits for them, and re-layouts  1.47 us (2%)
    pallas_call x1, Pallas kernels, shards(): pl.pallas_call(kernel, out_shape=jax.ShapeDtypeStruct((TOK, COLS), BF16),...  74 us

profile of v7, /device:TPU:72, one launch (start us, length us, event | category | flops | bytes accessed | tf_op | source)
XLA Modules:
  0.0 75.5 jit_solution(6452708351689831086)
XLA Ops:
  0.0 74.0 %shard_map.82 = bf16[128,256]{1,0:T(8,128)(2,1)} custom-call(bf16[6,4,128]{2,1,0:T(4,128)(2,1)} %pix_in.1, bf16[6,4,4096]{2,1,0:T(4,128)(2,1)} %emb_in.1, bf16[6,4096]{1,0:T(8,128)(2,1)} %bias_in.1, s32[96]{0:T(128)} %mask_in.1, bf16[256]{0:T(256)(128)(2,1)} %query_in.1, bf16[4096]{0:T(1024)(128)(2,1)} %gain_in.1, bf16[128,512]{1,0:T(8,128)(2,1)} %up_in.1, ...), custom_call_target="tpu_custom_call" | custom-call | tf_op jit(solution)/shard_map/pallas_call | solution.py:453
  74.0 1.5 %copy.10 = bf16[128,256]{1,0:T(8,128)(2,1)} copy(bf16[128,256]{1,0:T(8,128)(2,1)} %shard_map.82) | data formatting | bytes 131072

commit v8 on v7

--- a/solution.py
+++ b/solution.py
@@ -19,7 +19,7 @@
 SPLIT = (4, 4)
 SPLIT_NEAR = (2, 2)
 ORDER = (
-    ("x0", 0), ("z0", 0), ("pack",), ("z0", 1), ("start",), ("x0", 1), ("tz",), ("z0", 2), ("X", 0, 0, 1, 1),
+    ("x0", 0), ("z0", 0), ("z0", 1), ("start",), ("x0", 1), ("tz",), ("z0", 2), ("X", 0, 0, 1, 1),
     ("X", 1, 0, -1, 0), ("Z", 0, 1, 3), ("py",), ("z0", 3), ("Z", 0, -1, 0), ("X", 1, 0, 1, 1), ("tx",),
     ("X", 0, 0, -1, 0), ("XR", 0, 0, 1), ("Z", 0, -1, 1), ("Z", 0, 1, 2), ("X", 0, 1, 1, 3), ("agg", 0),
     ("XR", 1, 0, 1), ("z1", 0), ("Z", 0, 1, 1), ("tsib", 1), ("tsib", -1), ("Z", 0, -1, 3), ("X", 0, -1, -1, 0),
@@ -123,10 +123,6 @@
     def sent(view, group):
         copy_of(view, view, group, next(iter(keys)), sibling).wait_send()
 
-    pl.semaphore_wait(barrier, len(peers))
-    for i in (6, 7):
-        locals_[i].wait()
-
 
     def pieces(m, a):
         return (SPLIT if a % 4 else SPLIT_NEAR)[m]
@@ -273,10 +269,6 @@
         if b == 0:
             recv(pat.at[0:3], "py")
             locals_[3].wait()
-            for ref, dim in ((collect, 1), (expand, 0)):
-                which, real = block_of(lax.broadcasted_iota(jnp.int32, ref.shape, dim))
-                own = (which == lax.broadcasted_iota(jnp.int32, ref.shape, 1 - dim)) & real
-                ref[...] = jnp.where(own, 1.0, 0.0).astype(BF16)
         recv(tab.at[other, quarter], ("ts", b % 4))
         points_f = pat[...].reshape(DEPTH, TOK).astype(F32)
         twice = jnp.concatenate([points_f, points_f], axis=1)
@@ -443,6 +435,14 @@
         "ds": down_sum,
         "fin": finish,
     }
+    pack()
+    for ref, dim in ((collect, 1), (expand, 0)):
+        which, real = block_of(lax.broadcasted_iota(jnp.int32, ref.shape, dim))
+        own = (which == lax.broadcasted_iota(jnp.int32, ref.shape, 1 - dim)) & real
+        ref[...] = jnp.where(own, 1.0, 0.0).astype(BF16)
+    pl.semaphore_wait(barrier, len(peers))
+    for i in (6, 7):
+        locals_[i].wait()
     for name, *rest in ORDER:
         steps[name](*rest)
     assert len(keys) <= N_RECV and len(groups) <= N_SENT

time: 75.7 us -> 75.9 us (level)
  no operation moved by 1% of the time
where the time goes in v8:
time: 75.9 us; the launch traced here: 75.7 us
  Pallas kernels  74.2 us (98%)
  local copies, waits for them, and re-layouts  1.47 us (2%)
    pallas_call x1, Pallas kernels, shards(): pl.pallas_call(kernel, out_shape=jax.ShapeDtypeStruct((TOK, COLS), BF16),...  74.2 us

profile of v8, /device:TPU:72, one launch (start us, length us, event | category | flops | bytes accessed | tf_op | source)
XLA Modules:
  0.0 75.7 jit_solution(4553833744148138354)
XLA Ops:
  0.0 74.2 %shard_map.82 = bf16[128,256]{1,0:T(8,128)(2,1)} custom-call(bf16[6,4,128]{2,1,0:T(4,128)(2,1)} %pix_in.1, bf16[6,4,4096]{2,1,0:T(4,128)(2,1)} %emb_in.1, bf16[6,4096]{1,0:T(8,128)(2,1)} %bias_in.1, s32[96]{0:T(128)} %mask_in.1, bf16[256]{0:T(256)(128)(2,1)} %query_in.1, bf16[4096]{0:T(1024)(128)(2,1)} %gain_in.1, bf16[128,512]{1,0:T(8,128)(2,1)} %up_in.1, ...), custom_call_target="tpu_custom_call" | custom-call | tf_op jit(solution)/shard_map/pallas_call | solution.py:453
  74.2 1.5 %copy.10 = bf16[128,256]{1,0:T(8,128)(2,1)} copy(bf16[128,256]{1,0:T(8,128)(2,1)} %shard_map.82) | data formatting | bytes 131072
